TPU v7x, 32 devices: a whole 2x2x4 slice. The times are simulated.
32 devices in a mesh: dp: 8 (over z, y), krow: 4 (over x, core).
Axes of the slice: x: 2, y: 2, z: 4, core: 2. Of those that a mesh axis runs over, the one named last changes fastest.
Arguments:
- tokens: bfloat16 [64, 512, 768], P('dp', 'krow'), may hold values from -6 to 6
- segment_ids: int32 [64, 512], P('dp'), may hold values from 0 to 7, never falling along the last dimension, each value on 1 to 256 neighbouring positions
- segment_live: int32 [64, 8], P('dp'), may hold values 0 or 1
- w_query: bfloat16 [768, 768], replicated, may hold values from -0.21875 to 0.21875
- b_query: bfloat16 [768], replicated, may hold values from -3 to 3
- w_key: bfloat16 [768, 768], replicated, may hold values from -0.21875 to 0.21875
- w_value: bfloat16 [768, 768], replicated, may hold values from -0.21875 to 0.21875
- w_out: bfloat16 [768, 768], replicated, may hold values from -0.875 to 0.875
- b_out: bfloat16 [768], replicated, may hold values from -3 to 3
- attn_gain: bfloat16 [768], replicated, may hold values from 0.25 to 1.75
- attn_shift: bfloat16 [768], replicated, may hold values from -2 to 2
- w_up: bfloat16 [768, 3072], replicated, may hold values from -0.21875 to 0.21875
- b_up: bfloat16 [3072], replicated, may hold values from -3 to 3
- w_down: bfloat16 [3072, 768], replicated, may hold values from -0.109375 to 0.109375
- b_down: bfloat16 [768], replicated, may hold values from -3 to 3
- ffn_gain: bfloat16 [768], replicated, may hold values from 0.25 to 1.75
- ffn_shift: bfloat16 [768], replicated, may hold values from -2 to 2
- compress: bfloat16 [256, 512], replicated, may hold values from -0.375 to 0.375
- cotangent: bfloat16 [64, 512, 768], P('dp', 'krow'), may hold values from -6 to 6
Outputs:
- output: float32 [64, 512, 768], P('dp', 'krow')
- grad_tokens: float32 [64, 512, 768], P('dp', 'krow')
- grad_w_query: float32 [768, 768], P('krow', 'dp')
- grad_b_query: float32 [768], replicated
- grad_w_key: float32 [768, 768], P('krow', 'dp')
- grad_w_value: float32 [768, 768], P('krow', 'dp')
- grad_w_out: float32 [768, 768], P('krow', 'dp')
- grad_b_out: float32 [768], replicated
- grad_attn_gain: float32 [768], replicated
- grad_attn_shift: float32 [768], replicated
- grad_w_up: float32 [768, 3072], P('krow', 'dp')
- grad_b_up: float32 [3072], replicated
- grad_w_down: float32 [3072, 768], P('krow', 'dp')
- grad_b_down: float32 [768], replicated
- grad_ffn_gain: float32 [768], replicated
- grad_ffn_shift: float32 [768], replicated
- grad_compress: float32 [256, 512], P('krow', 'dp')
Inputs may be any that keep to these rules, and one draw needn't show every extreme that they name: `segment_ids`: segment numbers never fall along a row; one segment of each row has exactly 256 positions.
All inputs are finite; a program needn't handle non-finite values. No bound on the sum of `segment_live` on one device may be relied on, other than what follows from the above.
Results may differ from a plain program's by a relative error of at most 0.024.
Values may be sent and summed in bfloat16 or wider, within the bound.
No kernel may reach another device: no remote copies, remote signals or barrier semaphores. Data moves between devices by JAX's collectives and lax.ppermute only.
A program may use at most 192 MiB of HBM per device.

v0:
```python
import math

import jax
import jax.numpy as jnp
from jax import lax
from jax.sharding import PartitionSpec as P

H = 12
HD = 64


def joined(value, axis, join):
    pieces = jax.tree.map(lambda part: lax.all_gather(part, axis), value)
    head = jax.tree.map(lambda part: part[0], pieces)
    tail = jax.tree.map(lambda part: part[1:], pieces)
    subtotal, _ = lax.scan(lambda subtotal, slab: (join(subtotal, slab), None), head, tail)
    return subtotal


def layer_norm(value, norm_gain, norm_shift):
    average = jnp.mean(value, axis=-1, keepdims=True)
    centred = value - average
    spread = jnp.mean(centred * centred, axis=-1, keepdims=True)
    return centred * lax.rsqrt(spread + 1e-05) * norm_gain + norm_shift


def gelu_exact(value):
    return jax.nn.gelu(value, approximate=False)


def merge_soft(first, second):
    top_value = jnp.maximum(first[0], second[0])
    total = first[1] * jnp.exp(first[0] - top_value) + second[1] * jnp.exp(second[0] - top_value)
    return (top_value, total)


def local(
    tokens,
    segment_ids,
    segment_live,
    w_query,
    b_query,
    w_key,
    w_value,
    w_out,
    b_out,
    attn_gain,
    attn_shift,
    w_up,
    b_up,
    w_down,
    b_down,
    ffn_gain,
    ffn_shift,
    compress,
    cotangent,
):
    f32 = jnp.float32
    bf16 = jnp.bfloat16
    n_rows, local_len, width = tokens.shape
    seq_len = segment_ids.shape[1]
    key_count = compress.shape[0]
    key_local = key_count // lax.axis_size("krow")
    position = lax.axis_index("krow")
    scale = 1.0 / math.sqrt(HD)
    labels = jnp.arange(segment_live.shape[1], dtype=jnp.int32)
    match = (segment_ids[:, :, None] == labels[None, None, :]).astype(f32)
    live = jnp.sum(match * segment_live[:, None, :].astype(f32), axis=-1)
    compress_rows = lax.dynamic_slice_in_dim(compress, position * key_local, key_local, 0)
    gathered = lax.all_gather(tokens, "krow", axis=1, tiled=True)
    masked = (gathered.astype(f32) * live[:, :, None]).astype(bf16)
    query = (
        jnp.einsum("rtd,de->rte", gathered, w_query, preferred_element_type=f32)
        + b_query.astype(f32)
    ).astype(bf16)
    packed = jnp.einsum("jt,rtd->rjd", compress_rows, masked, preferred_element_type=f32).astype(
        bf16
    )
    keys = jnp.einsum("rjd,de->rje", packed, w_key, preferred_element_type=f32).astype(bf16)
    values = jnp.einsum("rjd,de->rje", packed, w_value, preferred_element_type=f32).astype(bf16)
    q_heads = query.reshape(n_rows, seq_len, H, HD)
    k_heads = keys.reshape(n_rows, key_local, H, HD)
    v_heads = values.reshape(n_rows, key_local, H, HD)
    scores = jnp.einsum("rihe,rjhe->rhij", q_heads, k_heads, preferred_element_type=f32) * scale
    local_top = jnp.max(scores, axis=-1)
    local_total = jnp.sum(jnp.exp(scores - local_top[..., None]), axis=-1)
    top_score, totals = joined((local_top, local_total), "krow", merge_soft)
    weights = jnp.exp(scores - top_score[..., None]) / totals[..., None]
    low_weights = weights.astype(bf16)
    partial_attn = jnp.einsum(
        "rhij,rjhe->rihe", low_weights, v_heads, preferred_element_type=f32
    ).reshape(n_rows, seq_len, width)
    attended = (
        lax.psum_scatter(partial_attn.astype(jnp.bfloat16), "krow", scatter_dimension=1, tiled=True)
        .astype(jnp.float32)
        .astype(bf16)
    )
    branch = jnp.einsum("rtd,de->rte", attended, w_out, preferred_element_type=f32) + b_out.astype(
        f32
    )
    hidden_one = tokens.astype(f32) + branch
    normed, norm_back = jax.vjp(
        layer_norm, hidden_one, attn_gain.astype(f32), attn_shift.astype(f32)
    )
    normed_low = normed.astype(bf16)
    upward = jnp.einsum("rtd,df->rtf", normed_low, w_up, preferred_element_type=f32) + b_up.astype(
        f32
    )
    activ, gelu_back = jax.vjp(gelu_exact, upward)
    activ_low = activ.astype(bf16)
    downward = jnp.einsum(
        "rtf,fd->rtd", activ_low, w_down, preferred_element_type=f32
    ) + b_down.astype(f32)
    output, final_back = jax.vjp(
        layer_norm, normed + downward, ffn_gain.astype(f32), ffn_shift.astype(f32)
    )
    d_hidden_two, g_ffn_gain, g_ffn_shift = final_back(cotangent.astype(f32))
    d_down = d_hidden_two.astype(bf16)
    g_w_down = jnp.einsum("rtf,rtd->fd", activ_low, d_down, preferred_element_type=f32)
    g_b_down = jnp.sum(d_down.astype(f32), axis=(0, 1))
    d_activ = jnp.einsum("rtd,fd->rtf", d_down, w_down, preferred_element_type=f32)
    (d_upward,) = gelu_back(d_activ)
    d_up_low = d_upward.astype(bf16)
    g_w_up = jnp.einsum("rtd,rtf->df", normed_low, d_up_low, preferred_element_type=f32)
    g_b_up = jnp.sum(d_up_low.astype(f32), axis=(0, 1))
    d_normed = d_hidden_two + jnp.einsum("rtf,df->rtd", d_up_low, w_up, preferred_element_type=f32)
    d_hidden_one, g_attn_gain, g_attn_shift = norm_back(d_normed)
    d_branch = d_hidden_one.astype(bf16)
    g_w_out = jnp.einsum("rtd,rte->de", attended, d_branch, preferred_element_type=f32)
    g_b_out = jnp.sum(d_branch.astype(f32), axis=(0, 1))
    d_attended = jnp.einsum("rte,de->rtd", d_branch, w_out, preferred_element_type=f32).astype(bf16)
    d_attn_full = lax.all_gather(d_attended, "krow", axis=1, tiled=True)
    da_heads = d_attn_full.reshape(n_rows, seq_len, H, HD)
    d_weights = jnp.einsum("rihe,rjhe->rhij", da_heads, v_heads, preferred_element_type=f32)
    row_dot = lax.psum(jnp.sum(weights * d_weights, axis=-1).astype(jnp.bfloat16), "krow").astype(
        jnp.float32
    )
    d_scores = (weights * (d_weights - row_dot[..., None])).astype(bf16)
    d_values = (
        jnp.einsum("rhij,rihe->rjhe", low_weights, da_heads, preferred_element_type=f32)
        .reshape(n_rows, key_local, width)
        .astype(bf16)
    )
    d_keys = (
        (jnp.einsum("rhij,rihe->rjhe", d_scores, q_heads, preferred_element_type=f32) * scale)
        .reshape(n_rows, key_local, width)
        .astype(bf16)
    )
    d_query_part = (
        jnp.einsum("rhij,rjhe->rihe", d_scores, k_heads, preferred_element_type=f32) * scale
    ).reshape(n_rows, seq_len, width)
    d_packed = (
        jnp.einsum("rje,de->rjd", d_keys, w_key, preferred_element_type=f32)
        + jnp.einsum("rje,de->rjd", d_values, w_value, preferred_element_type=f32)
    ).astype(bf16)
    g_w_key = jnp.einsum("rjd,rje->de", packed, d_keys, preferred_element_type=f32)
    g_w_value = jnp.einsum("rjd,rje->de", packed, d_values, preferred_element_type=f32)
    g_compress_part = jnp.einsum("rjd,rtd->jt", d_packed, masked, preferred_element_type=f32)
    d_tokens_part = (
        jnp.einsum("jt,rjd->rtd", compress_rows, d_packed, preferred_element_type=f32)
        * live[:, :, None]
    )
    d_query_local, d_tokens_local = (
        lax.psum_scatter(
            d_query_part.astype(jnp.bfloat16), "krow", scatter_dimension=1, tiled=True
        ).astype(jnp.float32),
        lax.psum_scatter(
            d_tokens_part.astype(jnp.bfloat16), "krow", scatter_dimension=1, tiled=True
        ).astype(jnp.float32),
    )
    d_query_low = d_query_local.astype(bf16)
    g_w_query = jnp.einsum("rtd,rte->de", tokens, d_query_low, preferred_element_type=f32)
    g_b_query = jnp.sum(d_query_low.astype(f32), axis=(0, 1))
    grad_tokens = (
        d_hidden_one
        + jnp.einsum("rte,de->rtd", d_query_low, w_query, preferred_element_type=f32)
        + d_tokens_local
    )
    section_one = (
        lax.psum_scatter(
            g_w_query.astype(jnp.bfloat16), "krow", scatter_dimension=0, tiled=True
        ).astype(jnp.float32),
        lax.psum_scatter(
            g_w_key.astype(jnp.bfloat16), "krow", scatter_dimension=0, tiled=True
        ).astype(jnp.float32),
        lax.psum_scatter(
            g_w_value.astype(jnp.bfloat16), "krow", scatter_dimension=0, tiled=True
        ).astype(jnp.float32),
        lax.psum_scatter(
            g_w_out.astype(jnp.bfloat16), "krow", scatter_dimension=0, tiled=True
        ).astype(jnp.float32),
        lax.psum_scatter(
            g_w_up.astype(jnp.bfloat16), "krow", scatter_dimension=0, tiled=True
        ).astype(jnp.float32),
        lax.psum_scatter(
            g_w_down.astype(jnp.bfloat16), "krow", scatter_dimension=0, tiled=True
        ).astype(jnp.float32),
    )
    matrices = (
        lax.psum_scatter(
            section_one[0].astype(jnp.bfloat16), "dp", scatter_dimension=1, tiled=True
        ).astype(jnp.float32),
        lax.psum_scatter(
            section_one[1].astype(jnp.bfloat16), "dp", scatter_dimension=1, tiled=True
        ).astype(jnp.float32),
        lax.psum_scatter(
            section_one[2].astype(jnp.bfloat16), "dp", scatter_dimension=1, tiled=True
        ).astype(jnp.float32),
        lax.psum_scatter(
            section_one[3].astype(jnp.bfloat16), "dp", scatter_dimension=1, tiled=True
        ).astype(jnp.float32),
        lax.psum_scatter(
            section_one[4].astype(jnp.bfloat16), "dp", scatter_dimension=1, tiled=True
        ).astype(jnp.float32),
        lax.psum_scatter(
            section_one[5].astype(jnp.bfloat16), "dp", scatter_dimension=1, tiled=True
        ).astype(jnp.float32),
        lax.psum_scatter(
            g_compress_part.astype(jnp.bfloat16), "dp", scatter_dimension=1, tiled=True
        ).astype(jnp.float32),
    )
    vectors = lax.psum(
        (g_b_query, g_b_out, g_attn_gain, g_attn_shift, g_b_up, g_b_down, g_ffn_gain, g_ffn_shift),
        ("dp", "krow"),
    )
    return (
        output,
        grad_tokens,
        matrices[0],
        vectors[0],
        matrices[1],
        matrices[2],
        matrices[3],
        vectors[1],
        vectors[2],
        vectors[3],
        matrices[4],
        vectors[4],
        matrices[5],
        vectors[5],
        vectors[6],
        vectors[7],
        matrices[6],
    )


def solution(mesh):
    in_specs = (
        P("dp", "krow", None),
        P("dp", None),
        P("dp", None),
        P(),
        P(),
        P(),
        P(),
        P(),
        P(),
        P(),
        P(),
        P(),
        P(),
        P(),
        P(),
        P(),
        P(),
        P(),
        P("dp", "krow", None),
    )
    out_specs = (
        P("dp", "krow", None),
        P("dp", "krow", None),
        P("krow", "dp"),
        P(),
        P("krow", "dp"),
        P("krow", "dp"),
        P("krow", "dp"),
        P(),
        P(),
        P(),
        P("krow", "dp"),
        P(),
        P("krow", "dp"),
        P(),
        P(),
        P(),
        P("krow", "dp"),
    )
    return jax.shard_map(local, mesh=mesh, in_specs=in_specs, out_specs=out_specs, check_vma=False)
```

profile of v0, /device:TPU:0, one launch (start us, length us, event | category | flops | bytes accessed | tf_op | source)
XLA Modules:
  0.0 1209.4 jit_solution(7265504280455716236)
XLA Ops:
  10.2 48.5 %all-gather.5.cloned.1.call-done = bf16[8,512,768]{2,1,0:T(8,128)(2,1)} async-done(((bf16[8,128,768]{2,1,0:T(8,128)(2,1)}), bf16[8,512,768]{2,1,0:T(8,128)(2,1)}) %all-gather.5.cloned.1.call-update) | async-done | bytes 6291472 | tf_op jit(solution)/shard_map/all_gather | solution.py:70
  66.3 9.7 add_convert_fusion.1
  103.3 8.9 all-gather
  118.4 11.7 convolution_convert_fusion
  130.1 9.2 copy.149
  147.5 57.8 %reduce-scatter.49.cloned.1.call-done = bf16[128,6144]{1,0:T(8,128)(2,1)} async-done(((bf16[512,6144]{1,0:T(8,128)(2,1)}), bf16[128,6144]{1,0:T(8,128)(2,1)}) %reduce-scatter.49.cloned.1.call-update) | async-done | bytes 1572880
  215.2 11.2 fusion.29
  226.4 30.0 %multiply_convert_fusion.3 = (bf16[8,128,3072]{2,1,0:T(8,128)(2,1)S(1)}, f32[8,128,3072]{2,1,0:T(8,128)}) fusion(f32[8,128,3072]{2,1,0:T(8,128)S(1)} %get-tuple-element.194, f32[3072]{0:T(1024)S(1)} %convert_element_type.225, u8[128,3072]{1,0:T(8,128)(4,1)S(1)} %get-tuple-element.148, u8[128,3072]{1,0:T(8,128)(4,1)S(1)} %get-tuple-element.147), kind=kLoop, calls=%fused_computation.22 | loop fusion | flops 223346688 | bytes 32256000 | tf_op jit(solution)/shard_map/convert_element_type | solution.py:110
  256.4 10.1 fusion.70
  274.4 18.9 %convert_reduce_fusion = (f32[3072]{0:T(1024)}, bf16[8,128,3072]{2,1,0:T(8,128)(2,1)}) fusion(f32[8,128,3072]{2,1,0:T(8,128)} %get-tuple-element.184, bf16[8,128,768]{2,1,0:T(8,128)(2,1)} %get-tuple-element.178, bf16[3072,768]{1,0:T(8,128)(2,1)} %param.34, f32[8,128,3072]{2,1,0:T(8,128)} %copy-done.8, f32[3072]{0:T(1024)S(1)} %convert_element_type.225), kind=kOutput, calls=%fused_computation.16 | convolution fusion | flops 4885312512 | bytes 37773312 | tf_op jit(solution)/shard_map/rtd,fd->rtf/dot_general | solution.py:121
  293.3 11.3 multiply_reduce_fusion.2
  312.3 46.5 %all-gather.7.cloned.1.call-done = bf16[8,512,768]{2,1,0:T(8,128)(2,1)} async-done(((bf16[8,128,768]{2,1,0:T(8,128)(2,1)}), bf16[8,512,768]{2,1,0:T(8,128)(2,1)}) %all-gather.7.cloned.1.call-update) | async-done | bytes 6291472 | tf_op jit(solution)/shard_map/all_gather | solution.py:132
  367.4 12.3 %multiply_reduce_fusion = (bf16[8,12,512]{2,1,0:T(8,128)(2,1)}, f32[8,12,512,64]{2,3,1,0:T(8,128)}) fusion(f32[8,12,512]{2,1,0:T(8,128)S(1)} %get-tuple-element.46, f32[8,12,512]{2,1,0:T(8,128)S(1)} %get-tuple-element.45, f32[8,12,512,64]{2,3,1,0:T(8,128)} %copy-done.1, bf16[8,512,12,64]{1,3,2,0:T(8,128)(2,1)} %bitcast.183, ...), kind=kOutput, calls=%fused_computation.20 | convolution fusion | flops 418332672 | bytes 32735232 | tf_op jit(solution)/shard_map/rihe,rjhe->rhij/dot_general | solution.py:134
  384.2 9.2 bitcast_convert_fusion
  393.4 10.8 bitcast_convert_fusion.1
  404.3 10.0 fusion.35
  419.1 11.5 multiply_convert_fusion.2
  444.5 9.7 copy.151
  473.6 16.3 %reduce-scatter.47.cloned.1.call-done = bf16[768,768]{1,0:T(8,128)(2,1)} async-done(((bf16[3072,768]{1,0:T(8,128)(2,1)}), bf16[768,768]{1,0:T(8,128)(2,1)}) %reduce-scatter.47.cloned.1.call-update) | async-done | bytes 1179664 | tf_op jit(solution)/shard_map/reduce_scatter | solution.py:195
  492.3 48.0 %reduce-scatter.45.cloned.1.call-done = bf16[192,3072]{1,0:T(8,128)(2,1)} async-done(((bf16[768,3072]{1,0:T(8,128)(2,1)}), bf16[192,3072]{1,0:T(8,128)(2,1)}) %reduce-scatter.45.cloned.1.call-update) | async-done | bytes 1179664 | tf_op jit(solution)/shard_map/reduce_scatter | solution.py:192
  542.9 25.9 %reduce-scatter.41.cloned.1.call-done = bf16[192,768]{1,0:T(8,128)(2,1)} async-done(((bf16[768,768]{1,0:T(8,128)(2,1)}), bf16[192,768]{1,0:T(8,128)(2,1)}) %reduce-scatter.41.cloned.1.call-update) | async-done | bytes 294928 | tf_op jit(solution)/shard_map/reduce_scatter | solution.py:186
  570.8 26.3 %reduce-scatter.39.cloned.1.call-done = bf16[192,768]{1,0:T(8,128)(2,1)} async-done(((bf16[768,768]{1,0:T(8,128)(2,1)}), bf16[192,768]{1,0:T(8,128)(2,1)}) %reduce-scatter.39.cloned.1.call-update) | async-done | bytes 294928 | tf_op jit(solution)/shard_map/reduce_scatter | solution.py:183
  599.1 59.0 %reduce-scatter.51.cloned.1.call-done = bf16[128,6144]{1,0:T(8,128)(2,1)} async-done(((bf16[512,6144]{1,0:T(8,128)(2,1)}), bf16[128,6144]{1,0:T(8,128)(2,1)}) %reduce-scatter.51.cloned.1.call-update) | async-done | bytes 1572880
  674.3 48.4 %reduce-scatter.59.cloned.1.call-done = bf16[96,192]{1,0:T(8,128)(2,1)} async-done(((bf16[768,192]{1,0:T(8,128)(2,1)}), bf16[96,192]{1,0:T(8,128)(2,1)}) %reduce-scatter.59.cloned.1.call-update) | async-done | bytes 36880
  724.3 62.1 %reduce-scatter.65.cloned.1.call-done = bf16[64,64]{1,0:T(8,128)(2,1)} async-done(((bf16[512,64]{1,0:T(8,128)(2,1)}), bf16[64,64]{1,0:T(8,128)(2,1)}) %reduce-scatter.65.cloned.1.call-update) | async-done | bytes 8208
  787.8 65.2 %reduce-scatter.63.cloned.1.call-done = bf16[96,768]{1,0:T(8,128)(2,1)} async-done(((bf16[768,768]{1,0:T(8,128)(2,1)}), bf16[96,768]{1,0:T(8,128)(2,1)}) %reduce-scatter.63.cloned.1.call-update) | async-done | bytes 147472
  855.0 65.2 %reduce-scatter.61.cloned.1.call-done = bf16[384,192]{1,0:T(8,128)(2,1)} async-done(((bf16[3072,192]{1,0:T(8,128)(2,1)}), bf16[384,192]{1,0:T(8,128)(2,1)}) %reduce-scatter.61.cloned.1.call-update) | async-done | bytes 147472
  922.0 62.0 %reduce-scatter.57.cloned.1.call-done = bf16[96,192]{1,0:T(8,128)(2,1)} async-done(((bf16[768,192]{1,0:T(8,128)(2,1)}), bf16[96,192]{1,0:T(8,128)(2,1)}) %reduce-scatter.57.cloned.1.call-update) | async-done | bytes 36880
  985.5 62.3 %reduce-scatter.55.cloned.1.call-done = bf16[96,192]{1,0:T(8,128)(2,1)} async-done(((bf16[768,192]{1,0:T(8,128)(2,1)}), bf16[96,192]{1,0:T(8,128)(2,1)}) %reduce-scatter.55.cloned.1.call-update) | async-done | bytes 36880
  1049.7 41.4 %all-reduce = (f32[768]{0:T(1024)}, f32[768]{0:T(1024)}, f32[768]{0:T(1024)}, f32[768]{0:T(1024)}, f32[3072]{0:T(1024)}, /*index=5*/f32[768]{0:T(1024)}, f32[768]{0:T(1024)}, f32[768]{0:T(1024)}) all-reduce(f32[768]{0:T(1024)S(1)} %convert_reduce_fusion.4, f32[768]{0:T(1024)S(1)} %copy-done.24, ...), channel_id=1, replica_groups=mesh['dp'=8,'krow'=4] {'dp','krow'}, use_global_device_ids=true, to_apply=%region_21.22 | all-reduce | flops 8448 | bytes 67584 | tf_op jit(solution)/shard_map/psum | solution.py:222
  1093.1 43.0 %reduce-scatter.35.cloned.1.call-done = bf16[8,128,768]{2,1,0:T(8,128)(2,1)} async-done(((bf16[8,512,768]{2,1,0:T(8,128)(2,1)}), bf16[8,128,768]{2,1,0:T(8,128)(2,1)}) %reduce-scatter.35.cloned.1.call-update) | async-done | bytes 1572880 | tf_op jit(solution)/shard_map/reduce_scatter | solution.py:167
  1141.9 59.2 %reduce-scatter.37.cloned.1.call-done = bf16[192,96]{0,1:T(8,128)(2,1)} async-done(((bf16[192,768]{0,1:T(8,128)(2,1)}), bf16[192,96]{0,1:T(8,128)(2,1)}) %reduce-scatter.37.cloned.1.call-update) | async-done | bytes 36880 | tf_op jit(solution)/shard_map/reduce_scatter | solution.py:200
  (218 shorter events, 173.8 us)
Async XLA Ops:
  7.2 59.1 %copy-start = (bf16[768,768]{1,0:T(8,128)(2,1)S(1)}, bf16[768,768]{1,0:T(8,128)(2,1)}, u32[]{:S(2)}) copy-start(bf16[768,768]{1,0:T(8,128)(2,1)} %param.24) | copy-start | bytes 3538948
  7.2 56.8 %copy-start.19 = (bf16[768,768]{1,0:T(8,128)(2,1)S(1)}, bf16[768,768]{1,0:T(8,128)(2,1)}, u32[]{:S(2)}) copy-start(bf16[768,768]{1,0:T(8,128)(2,1)} %param.26) | copy-start | bytes 3538948
  7.2 51.5 %all-gather.5.cloned.1.call-start = ((), (), s32[]{:S(2)}) async-start(), calls=%async_computation.16 | async-start | bytes 7864320 | tf_op jit(solution)/shard_map/all_gather | solution.py:70
  8.0 197.4 %reduce-scatter.49.cloned.1.call-start = ((), (), s32[]{:S(2)}) async-start(), calls=%async_computation.26 | async-start | bytes 7864320
  10.2 48.5 %copy-start.20 = (f32[8,512]{1,0:T(8,128)}, f32[8,512]{1,0:T(8,128)S(1)}, u32[]{:S(2)}) copy-start(f32[8,512]{1,0:T(8,128)S(1)} %select_reduce_fusion) | copy-start | bytes 49156
  113.7 290.6 %copy-start.7 = (f32[8,12,512]{2,1,0:T(8,128)}, f32[8,12,512]{2,1,0:T(8,128)S(1)}, u32[]{:S(2)}) copy-start(f32[8,12,512]{2,1,0:T(8,128)S(1)} %get-tuple-element.45) | copy-start | bytes 589828
  146.8 64.3 %copy-start.17 = (bf16[768,768]{1,0:T(8,128)(2,1)S(1)}, bf16[768,768]{1,0:T(8,128)(2,1)}, u32[]{:S(2)}) copy-start(bf16[768,768]{1,0:T(8,128)(2,1)} %param.28) | copy-start | bytes 3538948
  146.8 212.1 %all-gather.7.cloned.1.call-start = ((), (), s32[]{:S(2)}) async-start(), calls=%async_computation.17 | async-start | bytes 7864320 | tf_op jit(solution)/shard_map/all_gather | solution.py:132
  312.3 105.9 %all-reduce.3.cloned.1.call-start = ((), (), s32[]{:S(2)}) async-start(), calls=%async_computation.18 | async-start | bytes 262144 | tf_op jit(solution)/shard_map/psum | solution.py:135
  379.7 82.2 %reduce-scatter.43.cloned.1.call-start = ((), (), s32[]{:S(2)}) async-start(), calls=%async_computation.23 | async-start | bytes 1474560 | tf_op jit(solution)/shard_map/reduce_scatter | solution.py:189
  384.2 105.7 %reduce-scatter.47.cloned.1.call-start = ((), (), s32[]{:S(2)}) async-start(), calls=%async_computation.25 | async-start | bytes 5898240 | tf_op jit(solution)/shard_map/reduce_scatter | solution.py:195
  393.4 146.9 %reduce-scatter.45.cloned.1.call-start = ((), (), s32[]{:S(2)}) async-start(), calls=%async_computation.24 | async-start | bytes 5898240 | tf_op jit(solution)/shard_map/reduce_scatter | solution.py:192
  404.3 164.5 %reduce-scatter.41.cloned.1.call-start = ((), (), s32[]{:S(2)}) async-start(), calls=%async_computation.22 | async-start | bytes 1474560 | tf_op jit(solution)/shard_map/reduce_scatter | solution.py:186
  418.1 179.0 %reduce-scatter.39.cloned.1.call-start = ((), (), s32[]{:S(2)}) async-start(), calls=%async_computation.21 | async-start | bytes 1474560 | tf_op jit(solution)/shard_map/reduce_scatter | solution.py:183
  437.0 221.1 %reduce-scatter.51.cloned.1.call-start = ((), (), s32[]{:S(2)}) async-start(), calls=%async_computation.27 | async-start | bytes 7864320
  461.9 260.8 %reduce-scatter.59.cloned.1.call-start = ((), (), s32[]{:S(2)}) async-start(), calls=%async_computation.31 | async-start | bytes 442368
  464.0 322.4 %reduce-scatter.65.cloned.1.call-start = ((), (), s32[]{:S(2)}) async-start(), calls=%async_computation.34 | async-start | bytes 147456
  473.5 379.5 %reduce-scatter.63.cloned.1.call-start = ((), (), s32[]{:S(2)}) async-start(), calls=%async_computation.33 | async-start | bytes 1327104
  492.3 427.9 %reduce-scatter.61.cloned.1.call-start = ((), (), s32[]{:S(2)}) async-start(), calls=%async_computation.32 | async-start | bytes 1769472
  542.9 441.1 %reduce-scatter.57.cloned.1.call-start = ((), (), s32[]{:S(2)}) async-start(), calls=%async_computation.30 | async-start | bytes 442368
  570.7 477.1 %reduce-scatter.55.cloned.1.call-start = ((), (), s32[]{:S(2)}) async-start(), calls=%async_computation.29 | async-start | bytes 442368
  599.0 492.2 %reduce-scatter.53.cloned.1.call-start = ((), (), s32[]{:S(2)}) async-start(), calls=%async_computation.28 | async-start | bytes 1474560
  669.3 466.8 %reduce-scatter.35.cloned.1.call-start = ((), (), s32[]{:S(2)}) async-start(), calls=%async_computation.19 | async-start | bytes 7864320 | tf_op jit(solution)/shard_map/reduce_scatter | solution.py:167
  674.0 375.7 %copy-start.22 = (f32[768]{0:T(1024)S(1)}, f32[768]{0:T(1024)}, u32[]{:S(2)}) copy-start(f32[768]{0:T(1024)} %get-tuple-element.177) | copy-start | bytes 9220
  674.0 375.7 %copy-start.23 = (f32[768]{0:T(1024)S(1)}, f32[768]{0:T(1024)}, u32[]{:S(2)}) copy-start(f32[768]{0:T(1024)} %get-tuple-element.151) | copy-start | bytes 9220
  674.0 375.7 %copy-start.24 = (f32[768]{0:T(1024)S(1)}, f32[768]{0:T(1024)}, u32[]{:S(2)}) copy-start(f32[768]{0:T(1024)} %get-tuple-element.179) | copy-start | bytes 9220
  674.0 375.7 %copy-start.27 = (f32[768]{0:T(1024)S(1)}, f32[768]{0:T(1024)}, u32[]{:S(2)}) copy-start(f32[768]{0:T(1024)} %get-tuple-element.156) | copy-start | bytes 9220
  674.0 375.7 %copy-start.28 = (f32[3072]{0:T(1024)S(1)}, f32[3072]{0:T(1024)}, u32[]{:S(2)}) copy-start(f32[3072]{0:T(1024)} %get-tuple-element.200) | copy-start | bytes 36868
  674.0 375.7 %copy-start.30 = (f32[768]{0:T(1024)S(1)}, f32[768]{0:T(1024)}, u32[]{:S(2)}) copy-start(f32[768]{0:T(1024)} %get-tuple-element.149) | copy-start | bytes 9220
  674.0 375.7 %copy-start.31 = (f32[768]{0:T(1024)S(1)}, f32[768]{0:T(1024)}, u32[]{:S(2)}) copy-start(f32[768]{0:T(1024)} %get-tuple-element.155) | copy-start | bytes 9220
  674.0 462.0 %copy-start.26 = (f32[8,128]{1,0:T(8,128)S(1)}, f32[8,128]{1,0:T(8,128)}, u32[]{:S(2)}) copy-start(f32[8,128]{1,0:T(8,128)} %copy-done.25) | copy-start | bytes 12292
  674.1 527.0 %reduce-scatter.37.cloned.1.call-start = ((), (), s32[]{:S(2)}) async-start(), calls=%async_computation.20 | async-start | bytes 442368 | tf_op jit(solution)/shard_map/reduce_scatter | solution.py:200
  (30 other events, 189.8 us)
Sparse Core Ops, SparseCore 0:
  9.6 49.0 all-gather.4
  146.9 58.4 reduce-scatter.48
  312.4 46.3 all-gather.6
  379.9 31.3 all-reduce.2
  413.7 25.7 reduce-scatter.42
  442.0 47.8 reduce-scatter.46
  492.4 47.8 reduce-scatter.44
  543.1 25.6 reduce-scatter.40
  571.3 25.7 reduce-scatter.38
  599.6 58.3 reduce-scatter.50
  661.4 61.3 reduce-scatter.58
  726.5 59.8 reduce-scatter.64
  789.8 63.1 reduce-scatter.62
  856.3 63.8 reduce-scatter.60
  923.6 60.2 reduce-scatter.56
  987.4 60.3 reduce-scatter.54
  1050.4 24.7 reduce-scatter.52
  1077.6 58.4 reduce-scatter.34
  1139.7 61.3 reduce-scatter.36
where the time goes:
time: 1220 us; the launch traced here: 1210 us
  waiting for transfers between devices  797 us (65%)
  matrix products  175 us (14%)
  local copies, waits for them, and re-layouts  98.3 us (8%)
  other arithmetic  63.5 us (5%)
  blocking collectives  59 us (5%)
  between operations  15 us (1%)
    unnamed x28, waiting for transfers between devices  483 us
    unnamed x110, local copies, waits for them, and re-layouts  76.5 us
    reduce_scatter x1, waiting for transfers between devices, local(): lax.psum_scatter(section_one[0].astype(jnp.bfloat16), 'dp', scatter_dimen...  59.2 us
    all_gather x1, waiting for transfers between devices, local(): gathered = lax.all_gather(tokens, 'krow', axis=1, tiled=True)  48.5 us
    reduce_scatter x1, waiting for transfers between devices, local(): lax.psum_scatter(g_w_up.astype(jnp.bfloat16), 'krow', scatter_dimension=0...  48 us
    all_gather x1, waiting for transfers between devices, local(): d_attn_full = lax.all_gather(d_attended, 'krow', axis=1, tiled=True)  46.5 us
    reduce_scatter x1, waiting for transfers between devices, local(): lax.psum_scatter(d_tokens_part.astype(jnp.bfloat16), 'krow', scatter_dime...  43 us
    psum x1, blocking collectives, local(): lax.psum((g_b_query, g_b_out, g_attn_gain, g_attn_shift, g_b_up, g_b_down...  41.4 us
  transfers between devices with their start and end apart: 19, of which 16 were waited for; matrix products, arithmetic and copies ran while one was open for 11% of the time, Pallas kernels for 0%

commit v1 on v0

v1 whole, which is shorter than its diff:
```python
import functools
import math

import jax
import jax.numpy as jnp
from jax import lax
from jax.experimental import pallas as pl
from jax.experimental.pallas import tpu as pltpu
from jax.sharding import PartitionSpec as P

H = 12
HD = 64
f32 = jnp.float32
bf16 = jnp.bfloat16
VMEM_LIMIT = 60 * 1024 * 1024


def nn(a, b):
    return lax.dot_general(a, b, (((1,), (0,)), ((), ())), preferred_element_type=f32)


def nt(a, b):
    return lax.dot_general(a, b, (((1,), (1,)), ((), ())), preferred_element_type=f32)


def whole(shape):
    rank = len(shape)
    return pl.BlockSpec(shape, lambda *_: (0,) * rank, pipeline_mode=pl.Buffered(1))


def row_block(*shape):
    rank = len(shape)
    return pl.BlockSpec((1,) + shape, lambda r, *_: (r,) + (0,) * rank)


def kernel_params(limit=VMEM_LIMIT):
    return pltpu.CompilerParams(dimension_semantics=("arbitrary",), vmem_limit_bytes=limit)


def cost(flops, moved, trans=0):
    return pl.CostEstimate(flops=int(flops), bytes_accessed=int(moved), transcendentals=int(trans))


def add_to(ref, value, first):
    @pl.when(first)
    def _():
        ref[...] = value

    @pl.when(jnp.logical_not(first))
    def _():
        ref[...] += value


def col_sum(value):
    return jnp.sum(value, axis=0, keepdims=True)


def gelu_parts(u):
    t = 1.0 / (1.0 + (0.3275911 / math.sqrt(2.0)) * jnp.abs(u))
    e = jnp.exp(-0.5 * u * u)
    poly = t * (
        0.5 * 0.254829592
        + t
        * (
            0.5 * -0.284496736
            + t * (0.5 * 1.421413741 + t * (0.5 * -1.453152027 + t * (0.5 * 1.061405429)))
        )
    )
    tail = poly * e
    phi = jnp.where(u > 0, 1.0 - tail, tail)
    return u * phi, phi + u * (e * (1.0 / math.sqrt(2.0 * math.pi)))


def attn_fwd_kernel(n, *refs):
    toks = refs[:n]
    live, comp, wq, bq, wk, wv, wo, bo = refs[n : n + 8]
    q_t, pk, k, v, lse, att, xhat, rstd = refs[n + 8 : n + 16]
    tok, att_t = refs[n + 16 :]
    length = toks[0].shape[1]
    for i in range(n):
        tok[i * length : (i + 1) * length, :] = toks[i][0]
    masked = (comp[...].astype(f32) * live[0]).astype(bf16)
    x = tok[...]
    pk[0] = nn(masked, x).astype(bf16)
    for c in range(3):
        cols = slice(256 * c, 256 * c + 256)
        q = (nn(x, wq[:, cols]) + bq[:, cols]).astype(bf16) * jnp.asarray(1.0 / math.sqrt(HD), bf16)
        q_t[0, cols, :] = q.T
        k[0, :, cols] = nn(pk[0], wk[:, cols]).astype(bf16)
        v[0, :, cols] = nn(pk[0], wv[:, cols]).astype(bf16)
    lane = lax.broadcasted_iota(jnp.int32, (1, 2 * HD), 1)
    for pair in range(H // 2):
        cols = slice(2 * HD * pair, 2 * HD * (pair + 1))
        k_pair = k[0, :, cols]
        v_t = v[0, :, cols].T
        for half in range(2):
            h = 2 * pair + half
            mine = jnp.where((lane // HD) == half, k_pair, jnp.zeros_like(k_pair))
            s = nn(mine, q_t[0, cols, :])
            top = jnp.max(s, axis=0, keepdims=True)
            e = jnp.exp(s - top)
            total = jnp.sum(e, axis=0, keepdims=True)
            w = (e * (1.0 / total)).astype(bf16)
            lse[0, h : h + 1, :] = top + jnp.log(total)
            att_t[h * HD : (h + 1) * HD, :] = nn(v_t[half * HD : (half + 1) * HD, :], w).astype(bf16)
    for c in range(3):
        cols = slice(256 * c, 256 * c + 256)
        att[0, :, cols] = att_t[cols, :].T
    hidden = x.astype(f32) + nn(att[0], wo[...]) + bo[...]
    average = jnp.mean(hidden, axis=-1, keepdims=True)
    centred = hidden - average
    spread = jnp.mean(centred * centred, axis=-1, keepdims=True)
    r = lax.rsqrt(spread + 1e-05)
    xhat[0] = centred * r
    rstd[0] = jnp.broadcast_to(r, rstd.shape[1:])


def attn_fwd(toks, live, comp, wq, bq, wk, wv, wo, bo):
    rows, length, width = toks[0].shape
    n = len(toks)
    seq = n * length
    keys = comp.shape[0]
    in_specs = [row_block(length, width)] * n + [
        row_block(1, seq),
        whole((keys, seq)),
        whole((width, width)),
        whole((1, width)),
        whole((width, width)),
        whole((width, width)),
        whole((width, width)),
        whole((1, width)),
    ]
    outs = [
        ((width, seq), bf16),
        ((keys, width), bf16),
        ((keys, width), bf16),
        ((keys, width), bf16),
        ((16, seq), f32),
        ((seq, width), bf16),
        ((seq, width), f32),
        ((seq, 128), f32),
    ]
    return pl.pallas_call(
        functools.partial(attn_fwd_kernel, n),
        grid=(rows,),
        in_specs=in_specs,
        out_specs=[row_block(*shape) for shape, _ in outs],
        out_shape=[jax.ShapeDtypeStruct((rows,) + shape, dt) for shape, dt in outs],
        scratch_shapes=[pltpu.VMEM((seq, width), bf16), pltpu.VMEM((width, seq), bf16)],
        compiler_params=kernel_params(),
        cost_estimate=cost(rows * 5e9, 12e6, rows * H * seq * keys),
        name="attn_fwd",
    )(*toks, live, comp, wq, bq, wk, wv, wo, bo)


class Places:
    def __init__(self, n_dp, n_krow):
        self.core = 2
        self.x = n_krow // 2
        self.y = n_krow // 2
        self.z = n_dp // self.y

    def shape(self, rows, cols):
        return (self.y, self.z, self.x, rows, cols)


def put_up(places, ids, nl_t, d_up, keep, send, temp):
    width = nl_t.shape[0]
    rows = width // (2 * places.x)
    cols = keep.shape[-1]
    step = cols * places.y
    for zr in range(places.z):
        start = pl.multiple_of((ids[2] ^ zr) * step, 128)
        temp[...] = nn(nl_t[...], d_up[:, pl.ds(start, step)])
        for cr, out in enumerate((keep, send)):
            for x in range(places.x):
                first = pl.multiple_of((2 * x + (ids[0] ^ cr)) * rows, 16)
                for y in range(places.y):
                    out[ids[1] ^ y, zr, ids[3] ^ x] = temp[
                        pl.ds(first, rows), y * cols : (y + 1) * cols
                    ].astype(bf16)


def put_down(places, ids, d_t, act, keep, send):
    width = d_t.shape[0]
    rows = keep.shape[-2]
    cols = keep.shape[-1]
    for cr, out in enumerate((keep, send)):
        for xr in range(places.x):
            start = pl.multiple_of((2 * (ids[3] ^ xr) + (ids[0] ^ cr)) * cols, 128)
            res = nn(d_t[...], act[:, pl.ds(start, cols)]).astype(bf16)
            for z in range(places.z):
                for y in range(places.y):
                    d = z * places.y + y
                    out[ids[1] ^ y, ids[2] ^ z, xr] = res[d * rows : (d + 1) * rows, :]


def put_square(places, ids, temp, keep, send, lead=()):
    rows = keep.shape[-2]
    cols = keep.shape[-1]
    for cr, out in enumerate((keep, send)):
        for z in range(places.z):
            for y in range(places.y):
                d = z * places.y + y
                first = pl.multiple_of(2 * rows * d + rows * (ids[0] ^ cr), 16)
                for x in range(places.x):
                    out[lead + (ids[1] ^ y, ids[2] ^ z, ids[3] ^ x)] = temp[
                        pl.ds(first, rows), x * cols : (x + 1) * cols
                    ].astype(bf16)


def ffn_fwd_kernel(n, places, ids, *refs):
    cots = refs[:n]
    xhat, gain, shift, wu, bu, wd, bd, fgain, fshift = refs[n : n + 9]
    refs = refs[n + 9 :]
    outs = refs[:n]
    gp, dh2, g_fgain, g_fshift, g_bd = refs[n : n + 5]
    grads = refs[n + 5 : -2]
    act, d_t = refs[-2:]
    r = pl.program_id(0)
    seq = xhat.shape[1]
    length = outs[0].shape[1]
    ff = wu.shape[1]
    chunk = 512
    rows = pl.ds(pl.multiple_of(r * seq, seq), seq)
    normed = xhat[0] * gain[...] + shift[...]
    low = normed.astype(bf16)
    total = normed + bd[...]
    for c in range(ff // chunk):
        cols = slice(c * chunk, (c + 1) * chunk)
        u = nn(low, wu[:, cols]) + bu[:, cols]
        a, g = gelu_parts(u)
        a = a.astype(bf16)
        act[rows, cols] = a
        gp[0, :, cols] = g.astype(bf16)
        total = total + nn(a, wd[cols, :])
    average = jnp.mean(total, axis=-1, keepdims=True)
    centred = total - average
    spread = jnp.mean(centred * centred, axis=-1, keepdims=True)
    rs = lax.rsqrt(spread + 1e-05)
    hat = centred * rs
    result = (hat * fgain[...] + fshift[...]).astype(bf16)
    for i in range(n):
        outs[i][0] = result[i * length : (i + 1) * length, :]
    cot = jnp.concatenate([c[0] for c in cots], axis=0).astype(f32)
    first = r == 0
    add_to(g_fgain, col_sum(cot * hat), first)
    add_to(g_fshift, col_sum(cot), first)
    dhat = cot * fgain[...]
    d = rs * (
        dhat
        - jnp.mean(dhat, axis=-1, keepdims=True)
        - hat * jnp.mean(dhat * hat, axis=-1, keepdims=True)
    )
    dh2[0] = d
    d_low = d.astype(bf16)
    add_to(g_bd, col_sum(d_low.astype(f32)), first)
    for i in range(pl.cdiv(d_t.shape[1], seq)):

        @pl.when(r == i)
        def _():
            d_t[:, i * seq : (i + 1) * seq] = d_low.T

    @pl.when(r == pl.num_programs(0) - 1)
    def _():
        if places is None:
            for c in range(ff // 768):
                cols = slice(c * 768, (c + 1) * 768)
                grads[0][:, cols] = nn(d_t[...], act[:, cols]).astype(bf16)
        else:
            put_down(places, ids, d_t, act, *grads)


def ffn_fwd(places, ids, cots, xhat, gain, shift, wu, bu, wd, bd, fgain, fshift):
    rows, length, width = cots[0].shape
    n = len(cots)
    seq = n * length
    ff = wu.shape[1]
    vec = whole((1, width))
    in_specs = (
        [pl.BlockSpec(memory_space=pltpu.SMEM)]
        + [row_block(length, width)] * n
        + [
            row_block(seq, width),
            vec,
            vec,
            whole((width, ff)),
            whole((1, ff)),
            whole((ff, width)),
            vec,
            vec,
            vec,
        ]
    )
    outs = [((length, width), bf16)] * n + [((seq, ff), bf16), ((seq, width), f32)]
    if places is None:
        grads = [(width, ff)]
    else:
        dp = places.y * places.z
        grads = [places.shape(width // dp, ff // (2 * places.x))] * 2
    return pl.pallas_call(
        functools.partial(ffn_fwd_kernel, n, places),
        grid=(rows,),
        in_specs=in_specs,
        out_specs=[row_block(*shape) for shape, _ in outs] + [vec] * 3 + [whole(g) for g in grads],
        out_shape=[jax.ShapeDtypeStruct((rows,) + shape, dt) for shape, dt in outs]
        + [jax.ShapeDtypeStruct((1, width), f32)] * 3
        + [jax.ShapeDtypeStruct(g, bf16) for g in grads],
        scratch_shapes=[
            pltpu.VMEM((rows * seq, ff), bf16),
            pltpu.VMEM((width, rows * seq), bf16),
        ],
        compiler_params=kernel_params(),
        cost_estimate=cost(rows * seq * width * ff * 6, 24e6, rows * seq * ff * 2),
        name="ffn_fwd",
    )(ids, *cots, xhat, gain, shift, wu, bu, wd, bd, fgain, fshift)


def ffn_bwd_kernel(places, ids, *refs):
    gp, dh2, xhat, rstd, att, gain, shift, wu, wd, wo = refs[:10]
    dh1, da_t, g_bu, g_gain, g_shift, g_bo = refs[10:16]
    split = 1 if places is None else 2
    up, out = refs[16 : 16 + split], refs[16 + split : 16 + 2 * split]
    dup, nl_t, gwo, temp = refs[16 + 2 * split :]
    r = pl.program_id(0)
    first = r == 0
    seq = xhat.shape[1]
    ff = wu.shape[1]
    chunk = 512
    rows = pl.ds(pl.multiple_of(r * seq, seq), seq)
    d_low = dh2[0].astype(bf16)
    dn = dh2[0]
    for c in range(ff // chunk):
        cols = slice(c * chunk, (c + 1) * chunk)
        d = (gp[0, :, cols].astype(f32) * nt(d_low, wd[cols, :])).astype(bf16)
        dup[rows, cols] = d
        dn = dn + nt(d, wu[:, cols])
        s = col_sum(d.astype(f32))

        @pl.when(first)
        def _():
            g_bu[:, cols] = s

        @pl.when(jnp.logical_not(first))
        def _():
            g_bu[:, cols] += s

    hat = xhat[0]
    add_to(g_gain, col_sum(dn * hat), first)
    add_to(g_shift, col_sum(dn), first)
    dhat = dn * gain[...]
    d = rstd[0, :, 0:1] * (
        dhat
        - jnp.mean(dhat, axis=-1, keepdims=True)
        - hat * jnp.mean(dhat * hat, axis=-1, keepdims=True)
    )
    dh1[0] = d
    branch = d.astype(bf16)
    add_to(g_bo, col_sum(branch.astype(f32)), first)
    da_t[0] = nt(wo[...], branch).astype(bf16)
    add_to(gwo, nn(branch.T, att[0]), first)
    low = (hat * gain[...] + shift[...]).astype(bf16)
    for i in range(pl.cdiv(nl_t.shape[1], seq)):

        @pl.when(r == i)
        def _():
            nl_t[:, i * seq : (i + 1) * seq] = low.T

    @pl.when(r == pl.num_programs(0) - 1)
    def _():
        if places is None:
            for c in range(ff // 768):
                cols = slice(c * 768, (c + 1) * 768)
                up[0][:, cols] = nn(nl_t[...], dup[:, cols]).astype(bf16)
            out[0][...] = gwo[...].astype(bf16)
        else:
            put_up(places, ids, nl_t, dup, *up, temp)
            put_square(places, ids, gwo, *out)


def ffn_bwd(places, ids, gp, dh2, xhat, rstd, att, gain, shift, wu, wd, wo):
    rows, seq, ff = gp.shape
    width = wu.shape[0]
    vec = whole((1, width))
    in_specs = [
        pl.BlockSpec(memory_space=pltpu.SMEM),
        row_block(seq, ff),
        row_block(seq, width),
        row_block(seq, width),
        row_block(seq, 128),
        row_block(seq, width),
        vec,
        vec,
        whole((width, ff)),
        whole((ff, width)),
        whole((width, width)),
    ]
    outs = [((seq, width), f32), ((width, seq), bf16)]
    if places is None:
        grads = [(width, ff), (width, width)]
    else:
        dp = places.y * places.z
        grads = [places.shape(width // (2 * places.x), ff // dp)] * 2
        grads += [places.shape(width // (2 * dp), width // places.x)] * 2
    return pl.pallas_call(
        functools.partial(ffn_bwd_kernel, places),
        grid=(rows,),
        in_specs=in_specs,
        out_specs=[row_block(*shape) for shape, _ in outs]
        + [whole((1, ff))]
        + [vec] * 3
        + [whole(g) for g in grads],
        out_shape=[jax.ShapeDtypeStruct((rows,) + shape, dt) for shape, dt in outs]
        + [jax.ShapeDtypeStruct((1, ff), f32)]
        + [jax.ShapeDtypeStruct((1, width), f32)] * 3
        + [jax.ShapeDtypeStruct(g, bf16) for g in grads],
        scratch_shapes=[
            pltpu.VMEM((rows * seq, ff), bf16),
            pltpu.VMEM((width, rows * seq), bf16),
            pltpu.VMEM((width, width), f32),
            pltpu.VMEM((width, width), f32),
        ],
        compiler_params=kernel_params(),
        cost_estimate=cost(rows * seq * width * ff * 6, 30e6),
        name="ffn_bwd",
    )(ids, gp, dh2, xhat, rstd, att, gain, shift, wu, wd, wo)


def attn_bwd_kernel(n, places, ids, *refs):
    toks = refs[:n]
    q_t, pk, k, v, lse, da_t, comp_t, live_row, live_col, wq, wk, wv, dh1 = refs[n : n + 13]
    refs = refs[n + 13 :]
    outs = refs[:n]
    g_bq = refs[n]
    split = 1 if places is None else 2
    square, small = refs[n + 1 : n + 1 + split], refs[n + 1 + split : n + 1 + 2 * split]
    tok, dq_t, dk_t, dv_t, gq, gk, gv, gc = refs[n + 1 + 2 * split :]
    length = toks[0].shape[1]
    r = pl.program_id(0)
    first = r == 0
    for i in range(n):
        tok[i * length : (i + 1) * length, :] = toks[i][0]
    lane = lax.broadcasted_iota(jnp.int32, (1, 2 * HD), 1)
    scale = jnp.asarray(1.0 / math.sqrt(HD), f32)
    for pair in range(H // 2):
        cols = slice(2 * HD * pair, 2 * HD * (pair + 1))
        k_pair = k[0, :, cols]
        v_pair = v[0, :, cols]
        k_t = k_pair.T
        for half in range(2):
            h = 2 * pair + half
            head = slice(h * HD, (h + 1) * HD)
            mine = (lane // HD) == half
            s = nn(jnp.where(mine, k_pair, jnp.zeros_like(k_pair)), q_t[0, cols, :])
            w = jnp.exp(s - lse[0, h : h + 1, :])
            dw = nn(jnp.where(mine, v_pair, jnp.zeros_like(v_pair)), da_t[0, cols, :])
            dot = jnp.sum(w * dw, axis=0, keepdims=True)
            ds = (w * (dw - dot)).astype(bf16)
            dv_t[head, :] = nt(da_t[0, head, :], w.astype(bf16)).astype(bf16)
            dk_t[head, :] = nt(q_t[0, head, :], ds).astype(bf16)
            dq_t[head, :] = (nn(k_t[half * HD : (half + 1) * HD, :], ds) * scale).astype(bf16)
    add_to(gk, nn(dk_t[...], pk[0]), first)
    add_to(gv, nn(dv_t[...], pk[0]), first)
    add_to(gq, nn(dq_t[...], tok[...]), first)
    dp_t = (nn(wk[...], dk_t[...]) + nn(wv[...], dv_t[...])).astype(bf16)
    add_to(gc, nn(tok[...], dp_t) * live_col[0, :, 0:1], first)
    masked = (comp_t[...].astype(f32) * live_col[0, :, 0:1]).astype(bf16)
    dq = dq_t[...].T
    add_to(g_bq, col_sum(dq.astype(f32)), first)
    grad = dh1[0] + nt(dq, wq[...]) + nt(masked, dp_t)
    for i in range(n):
        outs[i][0] = grad[i * length : (i + 1) * length, :].astype(bf16)

    @pl.when(r == pl.num_programs(0) - 1)
    def _():
        for i, g in enumerate((gq, gk, gv)):
            if places is None:
                square[0][i] = g[...].astype(bf16)
            else:
                put_square(places, ids, g, *square, lead=(i,))
        if places is None:
            small[0][...] = gc[...].astype(bf16)
        else:
            rows, cols = small[0].shape[-2:]
            for cr, out in enumerate(small):
                for i in range(n):
                    for j in range(length // (2 * rows)):
                        d = (ids[4] ^ i) * (length // (2 * rows)) + j
                        y, z = d % places.y, d // places.y
                        start = pl.multiple_of(i * length + 2 * rows * j + rows * (ids[0] ^ cr), 16)
                        for x in range(places.x):
                            out[ids[1] ^ y, ids[2] ^ z, ids[3] ^ x] = gc[
                                pl.ds(start, rows), x * cols : (x + 1) * cols
                            ].astype(bf16)


def attn_bwd(places, ids, toks, q_t, pk, k, v, lse, da_t, comp_t, live_row, live_col, wq, wk, wv, dh1):
    rows, length, width = toks[0].shape
    n = len(toks)
    seq = n * length
    keys = comp_t.shape[1]
    in_specs = (
        [pl.BlockSpec(memory_space=pltpu.SMEM)]
        + [row_block(length, width)] * n
        + [
            row_block(width, seq),
            row_block(keys, width),
            row_block(keys, width),
            row_block(keys, width),
            row_block(16, seq),
            row_block(width, seq),
            whole((seq, keys)),
            row_block(1, seq),
            row_block(seq, 128),
            whole((width, width)),
            whole((width, width)),
            whole((width, width)),
            row_block(seq, width),
        ]
    )
    outs = [((length, width), bf16)] * n
    if places is None:
        grads = [(3, width, width), (seq, keys)]
    else:
        dp = places.y * places.z
        grads = [(3,) + places.shape(width // (2 * dp), width // places.x)] * 2
        grads += [places.shape(seq // (2 * dp), keys // places.x)] * 2
    return pl.pallas_call(
        functools.partial(attn_bwd_kernel, n, places),
        grid=(rows,),
        in_specs=in_specs,
        out_specs=[row_block(*shape) for shape, _ in outs]
        + [whole((1, width))]
        + [whole(g) for g in grads],
        out_shape=[jax.ShapeDtypeStruct((rows,) + shape, dt) for shape, dt in outs]
        + [jax.ShapeDtypeStruct((1, width), f32)]
        + [jax.ShapeDtypeStruct(g, bf16) for g in grads],
        scratch_shapes=[
            pltpu.VMEM((seq, width), bf16),
            pltpu.VMEM((width, seq), bf16),
            pltpu.VMEM((width, keys), bf16),
            pltpu.VMEM((width, keys), bf16),
            pltpu.VMEM((width, width), f32),
            pltpu.VMEM((width, width), f32),
            pltpu.VMEM((width, width), f32),
            pltpu.VMEM((seq, keys), f32),
        ],
        compiler_params=kernel_params(),
        cost_estimate=cost(rows * 9e9, 20e6, rows * H * seq * keys),
        name="attn_bwd",
    )(ids, *toks, q_t, pk, k, v, lse, da_t, comp_t, live_row, live_col, wq, wk, wv, dh1)


def gather_rows_kernel(n, ids, *refs):
    out = refs[n]
    for i in range(n):

        @pl.when(pl.program_id(0) == i)
        def _():
            out[...] = refs[i][...].astype(f32)


def gather_rows(ids, parts):
    n = len(parts)
    rows, length, width = parts[0].shape
    spec = pl.BlockSpec((rows, length, width), lambda i, ids: (0, 0, 0))
    return pl.pallas_call(
        functools.partial(gather_rows_kernel, n),
        grid_spec=pltpu.PrefetchScalarGridSpec(
            num_scalar_prefetch=1,
            grid=(n,),
            in_specs=[spec] * n,
            out_specs=pl.BlockSpec((rows, length, width), lambda i, ids: (ids[4] ^ i, 0, 0)),
        ),
        out_shape=jax.ShapeDtypeStruct((n * rows, length, width), f32),
        compiler_params=kernel_params(32 * 1024 * 1024),
        cost_estimate=cost(0, 6 * n * rows * length * width),
        name="gather_rows",
    )(ids, *parts)


def exchange(value, axis, size, relative):
    pairs = [(i, i ^ relative) for i in range(size)]
    return lax.ppermute(value, axis, pairs)


def total_of(parts):
    acc = parts[0].astype(f32)
    for part in parts[1:]:
        acc = acc + part.astype(f32)
    return acc


def reduce_blocks(places, n_dp, n_krow, keep, send, lead=0):
    at = (slice(None),) * lead
    came = exchange(send, "krow", n_krow, 1)
    parts = []
    for yr in range(places.y):
        parts.append((keep[at + (yr,)].astype(f32) + came[at + (yr,)].astype(f32)).astype(bf16))
    got = [parts[0]]
    for yr in range(1, places.y):
        got.append(exchange(parts[yr], "dp", n_dp, yr))
    got = [
        total_of([g[at + (zr,)] for g in got]).astype(bf16) for zr in range(places.z)
    ]
    mine = [got[0]]
    for zr in range(1, places.z):
        mine.append(exchange(got[zr], "dp", n_dp, zr * places.y))
    return total_of(mine).astype(bf16)


def finish_blocks(places, n_krow, part, lead=0):
    at = (slice(None),) * lead
    got = [part[at + (0,)]]
    for xr in range(1, places.x):
        got.append(exchange(part[at + (xr,)], "krow", n_krow, 2 * xr))
    return total_of(got)


def finish_square(places, n_krow, core, part, lead=0):
    at = (slice(None),) * lead
    cols = part.shape[-1] // 2
    mine = lax.dynamic_slice_in_dim(part, core * cols, cols, part.ndim - 1)
    other = lax.dynamic_slice_in_dim(part, (1 - core) * cols, cols, part.ndim - 1)
    here, there = [mine[at + (0,)]], [exchange(other[at + (0,)], "krow", n_krow, 1)]
    for xr in range(1, places.x):
        here.append(exchange(mine[at + (xr,)], "krow", n_krow, 2 * xr))
        there.append(exchange(other[at + (xr,)], "krow", n_krow, 2 * xr + 1))
    here, there = total_of(here), total_of(there)
    low = jnp.where(core == 0, here, there)
    high = jnp.where(core == 0, there, here)
    return jnp.swapaxes(jnp.concatenate([low, high], axis=lead), -1, -2)


def local(
    sizes,
    tokens,
    segment_ids,
    segment_live,
    w_query,
    b_query,
    w_key,
    w_value,
    w_out,
    b_out,
    attn_gain,
    attn_shift,
    w_up,
    b_up,
    w_down,
    b_down,
    ffn_gain,
    ffn_shift,
    compress,
    cotangent,
):
    n_dp, n_krow = sizes
    all_rows, length, width = tokens.shape
    rows = all_rows // n_krow
    seq = n_krow * length
    keys = compress.shape[0]
    ff = w_up.shape[1]
    krow, dp = lax.axis_index("krow"), lax.axis_index("dp")
    places = Places(n_dp, n_krow)
    ids = jnp.stack([krow % 2, dp % places.y, dp // places.y, krow // 2, krow]).astype(jnp.int32)
    fast = (
        width % (2 * places.x * 16) == 0
        and ff % (n_dp * 128) == 0
        and ff % (n_krow * 128) == 0
        and width % (2 * n_dp * 16) == 0
        and seq % (2 * n_dp * 16) == 0
        and width % (places.x * 128) == 0
        and keys % (places.x * 128) == 0
        and length % (seq // n_dp) == 0
    )
    where = places if fast else None

    def spread(value):
        parts = []
        for r in range(n_krow):
            part = lax.dynamic_slice_in_dim(value, (krow ^ r) * rows, rows, 0)
            parts.append(exchange(part, "krow", n_krow, r) if r else part)
        return parts

    def back(parts):
        got = [exchange(part, "krow", n_krow, r) if r else part for r, part in enumerate(parts)]
        return gather_rows(ids, got)

    def row(value):
        return value.astype(f32).reshape(1, -1)

    toks = spread(tokens)
    cot_source = lax.optimization_barrier((cotangent, toks[-1]))[0]
    cots = spread(cot_source)

    my_ids = lax.dynamic_slice_in_dim(segment_ids, krow * rows, rows, 0)
    my_live = lax.dynamic_slice_in_dim(segment_live, krow * rows, rows, 0)
    labels = jnp.arange(segment_live.shape[1], dtype=jnp.int32)
    live = jnp.sum(
        jnp.where(my_ids[:, :, None] == labels, my_live[:, None, :], 0).astype(f32), axis=-1
    )

    def relative(value, axis):
        return jnp.concatenate(
            [
                lax.dynamic_slice_in_dim(value, (krow ^ r) * length, length, axis)
                for r in range(n_krow)
            ],
            axis=axis,
        )

    live = relative(live, 1)
    comp = relative(compress, 1)
    live_row = live[:, None, :]
    live_col = jnp.broadcast_to(live[:, :, None], (rows, seq, 128))

    q_t, pk, k, v, lse, att, xhat, rstd = attn_fwd(
        toks, live_row, comp, w_query, row(b_query), w_key, w_value, w_out, row(b_out)
    )
    gain, shift = row(attn_gain), row(attn_shift)
    res = ffn_fwd(
        where, ids, cots, xhat, gain, shift, w_up, row(b_up), w_down, row(b_down),
        row(ffn_gain), row(ffn_shift),
    )
    outs, (gp, dh2, g_fgain, g_fshift, g_bd), g_down = (
        res[:n_krow],
        res[n_krow : n_krow + 5],
        res[n_krow + 5 :],
    )
    res = ffn_bwd(where, ids, gp, dh2, xhat, rstd, att, gain, shift, w_up, w_down, w_out)
    dh1, da_t, g_bu, g_gain, g_shift, g_bo = res[:6]
    split = 2 if fast else 1
    g_up, g_out = res[6 : 6 + split], res[6 + split :]
    res = attn_bwd(
        where, ids, toks, q_t, pk, k, v, lse, da_t, comp.T, live_row, live_col,
        w_query, w_key, w_value, dh1,
    )
    grads, g_bq = res[:n_krow], res[n_krow]
    g_square, g_comp = res[n_krow + 1 : n_krow + 1 + split], res[n_krow + 1 + split :]

    output = back(outs)
    grad_tokens = back(grads)

    vectors = jnp.concatenate(
        [v.reshape(-1) for v in (g_bq, g_bo, g_gain, g_shift, g_bu, g_bd, g_fgain, g_fshift)]
    ).reshape(-1, 128)
    if fast:
        vectors = vectors + exchange(vectors, "krow", n_krow, 1)
        for size, step, axis, count in (
            (places.x, 2, "krow", n_krow),
            (places.y, 1, "dp", n_dp),
            (places.z, places.y, "dp", n_dp),
        ):
            vectors = total_of(
                [exchange(vectors, axis, count, step * r) if r else vectors for r in range(size)]
            )
        core = krow % 2
        down = finish_blocks(places, n_krow, reduce_blocks(places, n_dp, n_krow, *g_down)).T
        up = finish_blocks(places, n_krow, reduce_blocks(places, n_dp, n_krow, *g_up))
        out = finish_square(places, n_krow, core, reduce_blocks(places, n_dp, n_krow, *g_out))
        square = finish_square(
            places, n_krow, core, reduce_blocks(places, n_dp, n_krow, *g_square, lead=1), lead=1
        )
        small = finish_square(places, n_krow, core, reduce_blocks(places, n_dp, n_krow, *g_comp))
    else:
        vectors = lax.psum(vectors, ("dp", "krow"))

        def scattered(value):
            part = lax.psum_scatter(value, "krow", scatter_dimension=value.ndim - 2, tiled=True)
            return lax.psum_scatter(
                part, "dp", scatter_dimension=value.ndim - 1, tiled=True
            ).astype(f32)

        down = scattered(g_down[0].T)
        up = scattered(g_up[0])
        out = scattered(g_out[0].T)
        square = jnp.stack([scattered(g_square[0][i].T) for i in range(3)])
        blocks = g_comp[0].reshape(n_krow, length, keys)
        blocks = jnp.concatenate(
            [lax.dynamic_slice_in_dim(blocks, krow ^ r, 1, 0) for r in range(n_krow)]
        )
        small = scattered(blocks.reshape(seq, keys).T)

    pieces = []
    start = 0
    for size in (width, width, width, width, ff, width, width, width):
        pieces.append(vectors.reshape(-1)[start : start + size])
        start += size
    return (
        output,
        grad_tokens,
        square[0],
        pieces[0],
        square[1],
        square[2],
        out,
        pieces[1],
        pieces[2],
        pieces[3],
        up,
        pieces[4],
        down,
        pieces[5],
        pieces[6],
        pieces[7],
        small,
    )


def solution(mesh):
    rows = P("dp", "krow", None)
    per_row = P("dp", None)
    block = P("krow", "dp")
    in_specs = (rows, per_row, per_row) + (P(),) * 15 + (rows,)
    out_specs = (
        (rows, rows, block, P(), block, block, block)
        + (P(),) * 3
        + (block, P(), block)
        + (P(),) * 3
        + (block,)
    )
    sizes = (mesh.shape["dp"], mesh.shape["krow"])
    return jax.shard_map(
        functools.partial(local, sizes),
        mesh=mesh,
        in_specs=in_specs,
        out_specs=out_specs,
        check_vma=False,
    )
```

time: 1220 us -> 349 us (0.29)
  waiting for transfers between devices: 797 us -> 117 us
  matrix products: 175 us -> 0 us
  Pallas kernels: 0 us -> 125 us
  local copies, waits for them, and re-layouts: 98.3 us -> 19.2 us
  blocking collectives: 59 us -> 0 us
  starting transfers between devices: 1.58 us -> 54.2 us
  other arithmetic: 63.5 us -> 24.8 us
  between operations: 15 us -> 1.87 us
    unnamed x28 -> x0, waiting for transfers between devices: 483 us -> none
    reduce_scatter x7 -> x0, waiting for transfers between devices: 219 us -> none  [the longest x1 59.2 us: local(): lax.psum_scatter(section_one[0].astype(jnp.bfloat16), 'dp', scatter_dimen...]
    dot_general x27 -> x0, matrix products: 175 us -> none  [the longest x1 18.9 us: local(): jnp.einsum('rtd,fd->rtf', d_down, w_down, preferred_element_type=f32)]
    pallas_call x0 -> x6, Pallas kernels: none -> 125 us  [the longest x1 36.9 us: ffn_bwd(): pl.pallas_call(functools.partial(ffn_bwd_kernel, places), grid=(rows,), i...]
    ppermute x0 -> x54, waiting for transfers between devices: none -> 117 us  [exchange(): return lax.ppermute(value, axis, pairs)]
    all_gather x2 -> x0, waiting for transfers between devices: 95 us -> none  [the longest x1 48.5 us: local(): gathered = lax.all_gather(tokens, 'krow', axis=1, tiled=True)]
    unnamed x110 -> x86, local copies, waits for them, and re-layouts: 76.5 us -> 6.55 us
    ppermute x0 -> x54, starting transfers between devices: none -> 54.2 us  [exchange(): return lax.ppermute(value, axis, pairs)]
  transfers between devices with their start and end apart: 19 -> 54, of which waited for: 16 -> 25; matrix products, arithmetic and copies ran while one was open for 11% -> 10% of each run, Pallas kernels for 0% -> 7%
where the time goes in v1:
time: 349 us; the launch traced here: 343 us
  Pallas kernels  125 us (36%)
  waiting for transfers between devices  117 us (34%)
  starting transfers between devices  54.2 us (16%)
  other arithmetic  24.8 us (7%)
  local copies, waits for them, and re-layouts  19.2 us (6%)
    ppermute x54, waiting for transfers between devices, exchange(): return lax.ppermute(value, axis, pairs)  117 us
    ppermute x54, starting transfers between devices, exchange(): return lax.ppermute(value, axis, pairs)  54.2 us
    pallas_call x1, Pallas kernels, ffn_bwd(): pl.pallas_call(functools.partial(ffn_bwd_kernel, places), grid=(rows,), i...  36.9 us
    pallas_call x1, Pallas kernels, ffn_fwd(): pl.pallas_call(functools.partial(ffn_fwd_kernel, n, places), grid=(rows,)...  36.4 us
    pallas_call x1, Pallas kernels, attn_bwd(): pl.pallas_call(functools.partial(attn_bwd_kernel, n, places), grid=(rows,...  28.7 us
    pallas_call x1, Pallas kernels, attn_fwd(): pl.pallas_call(functools.partial(attn_fwd_kernel, n), grid=(rows,), in_sp...  17.8 us
    convert_element_type x6, other arithmetic, reduce_blocks(): (keep[at + (yr,)].astype(f32) + came[at + (yr,)].astype(f32)).astype(bf16)  9.46 us
  transfers between devices with their start and end apart: 54, of which 25 were waited for; matrix products, arithmetic and copies ran while one was open for 10% of the time, Pallas kernels for 7%

profile of v1, /device:TPU:0, one launch (start us, length us, event | category | flops | bytes accessed | tf_op | source)
XLA Modules:
  0.0 342.6 jit_solution(3798592827323364974)
XLA Ops:
  0.8 2.3 constant_dynamic-slice_fusion.10
  3.1 2.9 collective-permute-start.5
  15.1 7.7 %collective-permute-done.refs_3_ = bf16[2,128,768]{2,1,0:T(8,128)(2,1)} collective-permute-done((bf16[2,128,768]{2,1,0:T(8,128)(2,1)S(1)}, bf16[2,128,768]{2,1,0:T(8,128)(2,1)}, u32[]{:S(2)}, u32[]{:S(2)}) %collective-permute-start) | collective-permute-done | bytes 393248 | tf_op jit(solution)/shard_map/ppermute | solution.py:584
  23.7 2.0 collective-permute-start.3
  26.0 17.8 %attn_fwd.1 = (bf16[2,768,512]{2,1,0:T(8,128)(2,1)}, bf16[2,256,768]{2,1,0:T(8,128)(2,1)}, bf16[2,256,768]{2,1,0:T(8,128)(2,1)}, bf16[2,256,768]{2,1,0:T(8,128)(...) custom-call(bf16[2,128,768]{2,1,0:T(8,128)(2,1)} %get-tuple-element., ...), custom_call_target="tpu_custom_call" | custom-call | flops 10000000000 | bytes 12000000 | tf_op jit(solution)/shard_map/attn_fwd/pallas_call | solution.py:143
  44.9 36.4 %ffn_fwd.1 = (bf16[2,128,768]{2,1,0:T(8,128)(2,1)}, bf16[2,128,768]{2,1,0:T(8,128)(2,1)}, bf16[2,128,768]{2,1,0:T(8,128)(2,1)}, bf16[2,128,768]{2,1,0:T(8,128)(2...) custom-call(s32[5]{0:T(128)} %stack.23.ids, ...), custom_call_target="tpu_custom_call" | custom-call | flops 14495514624 | bytes 24000000 | tf_op jit(solution)/shard_map/ffn_fwd/pallas_call | solution.py:301
  83.4 36.9 %ffn_bwd.1 = (f32[2,512,768]{2,1,0:T(8,128)}, bf16[2,768,512]{2,1,0:T(8,128)(2,1)}, f32[1,3072]{1,0:T(1,128)}, f32[1,768]{1,0:T(1,128)}, f32[1,768]{1,0:T(1,128)...) custom-call(s32[5]{0:T(128)} %stack.23.ids, ...), custom_call_target="tpu_custom_call" | custom-call | flops 14495514624 | bytes 30000000 | tf_op jit(solution)/shard_map/ffn_bwd/pallas_call | solution.py:405
  121.2 28.7 %attn_bwd.1 = (bf16[2,128,768]{2,1,0:T(8,128)(2,1)}, bf16[2,128,768]{2,1,0:T(8,128)(2,1)}, bf16[2,128,768]{2,1,0:T(8,128)(2,1)}, bf16[2,128,768]{2,1,0:T(8,128)(...) custom-call(s32[5]{0:T(128)} %stack.23.ids, ...), custom_call_target="tpu_custom_call" | custom-call | flops 17999998976 | bytes 20000000 | tf_op jit(solution)/shard_map/attn_bwd/pallas_call | solution.py:528
  161.4 2.5 collective-permute-start.50
  164.1 3.1 collective-permute-start.25
  172.9 3.1 collective-permute-done.51
  177.9 9.0 %collective-permute-done.53 = bf16[32,64]{1,0:T(8,128)(2,1)S(1)} collective-permute-done((bf16[32,64]{1,0:T(8,128)(2,1)S(1)}, bf16[32,64]{1,0:T(8,128)(2,1)S(1)}, u32[]{:S(2)}, u32[]{:S(2)}) %collective-permute-start.53) | collective-permute-done | bytes 4128 | tf_op jit(solution)/shard_map/ppermute | solution.py:584
  194.8 3.8 %collective-permute-done.29 = bf16[2,48,384]{2,1,0:T(8,128)(2,1)S(1)} collective-permute-done((bf16[2,48,384]{2,1,0:T(8,128)(2,1)S(1)}, bf16[2,48,384]{2,1,0:T(8,128)(2,1)S(1)}, u32[]{:S(2)}, u32[]{:S(2)}) %collective-permute-start.29) | collective-permute-done | bytes 73760 | tf_op jit(solution)/shard_map/ppermute | solution.py:584
  198.8 6.8 %collective-permute-done.8.refs_3_ = bf16[2,128,768]{2,1,0:T(8,128)(2,1)S(1)} collective-permute-done((bf16[2,128,768]{2,1,0:T(8,128)(2,1)S(1)}, bf16[2,128,768]{2,1,0:T(8,128)(2,1)S(1)}, u32[]{:S(2)}, u32[]{:S(2)}) %collective-permute-start.8) | collective-permute-done | bytes 393248 | tf_op jit(solution)/shard_map/ppermute | solution.py:584
  209.5 8.3 %collective-permute-done.10.refs_2_ = bf16[2,128,768]{2,1,0:T(8,128)(2,1)S(1)} collective-permute-done((bf16[2,128,768]{2,1,0:T(8,128)(2,1)}, bf16[2,128,768]{2,1,0:T(8,128)(2,1)S(1)}, u32[]{:S(2)}, u32[]{:S(2)}) %collective-permute-start.10) | collective-permute-done | bytes 393248 | tf_op jit(solution)/shard_map/ppermute | solution.py:584
  217.8 6.4 %collective-permute-done.11.refs_3_ = bf16[2,128,768]{2,1,0:T(8,128)(2,1)S(1)} collective-permute-done((bf16[2,128,768]{2,1,0:T(8,128)(2,1)S(1)}, bf16[2,128,768]{2,1,0:T(8,128)(2,1)S(1)}, u32[]{:S(2)}, u32[]{:S(2)}) %collective-permute-start.11) | collective-permute-done | bytes 393248 | tf_op jit(solution)/shard_map/ppermute | solution.py:584
  227.9 2.7 gather_rows.2
  230.6 2.7 gather_rows.3
  235.0 3.6 %add_convert_fusion.1 = (bf16[1,4,2,96,768]{4,3,2,1,0:T(8,128)(2,1)S(1)}, bf16[4,2,96,768]{3,2,1,0:T(8,128)(2,1)}) fusion(bf16[2,4,2,96,768]{4,3,2,1,0:T(8,128)(2,1)} %collective-permute-done.40, bf16[2,4,2,96,768]{4,3,2,1,0:T(8,128)(2,1)S(1)} %copy-done.6), kind=kLoop, calls=%fused_computation.1 | loop fusion | flops 4718592 | bytes 7077888 | tf_op jit(solution)/shard_map/convert_element_type | solution.py:599
  239.5 9.5 %collective-permute-done.13 = bf16[3,4,2,48,384]{4,3,2,1,0:T(8,128)(2,1)} collective-permute-done((bf16[3,4,2,48,384]{4,3,2,1,0:T(8,128)(2,1)}, bf16[3,4,2,48,384]{4,3,2,1,0:T(8,128)(2,1)}, u32[]{:S(2)}, u32[]{:S(2)}) %collective-permute-start.13) | collective-permute-done | bytes 884768 | tf_op jit(solution)/shard_map/ppermute | solution.py:584
  253.1 2.3 collective-permute-start.14
  255.8 3.3 add_convert_fusion.3
  262.2 8.1 %collective-permute-done.15 = bf16[3,2,48,384]{3,2,1,0:T(8,128)(2,1)S(1)} collective-permute-done((bf16[3,2,48,384]{3,2,1,0:T(8,128)(2,1)S(1)}, bf16[3,2,48,384]{3,2,1,0:T(8,128)(2,1)S(1)}, u32[]{:S(2)}, u32[]{:S(2)}) %collective-permute-start.15) | collective-permute-done | bytes 221216 | tf_op jit(solution)/shard_map/ppermute | solution.py:584
  277.1 2.2 fusion.28
  279.4 2.1 collective-permute-start.44
  285.0 13.0 %collective-permute-done.35 = bf16[4,2,192,384]{3,2,1,0:T(8,128)(2,1)} collective-permute-done((bf16[4,2,192,384]{3,2,1,0:T(8,128)(2,1)}, bf16[4,2,192,384]{3,2,1,0:T(8,128)(2,1)}, u32[]{:S(2)}, u32[]{:S(2)}) %collective-permute-start.35) | collective-permute-done | bytes 1179680 | tf_op jit(solution)/shard_map/ppermute | solution.py:584
  299.3 3.1 collective-permute-start.36
  302.4 2.3 collective-permute-start.38
  304.7 6.5 %collective-permute-done.43 = bf16[2,96,768]{2,1,0:T(8,128)(2,1)S(1)} collective-permute-done((bf16[2,96,768]{2,1,0:T(8,128)(2,1)}, bf16[2,96,768]{2,1,0:T(8,128)(2,1)S(1)}, u32[]{:S(2)}, u32[]{:S(2)}) %collective-permute-start.43) | collective-permute-done | bytes 294944 | tf_op jit(solution)/shard_map/ppermute | solution.py:584
  313.5 7.2 %collective-permute-done.36 = bf16[2,192,384]{2,1,0:T(8,128)(2,1)S(1)} collective-permute-done((bf16[2,192,384]{2,1,0:T(8,128)(2,1)S(1)}, bf16[2,192,384]{2,1,0:T(8,128)(2,1)S(1)}, u32[]{:S(2)}, u32[]{:S(2)}) %collective-permute-start.36) | collective-permute-done | bytes 294944 | tf_op jit(solution)/shard_map/ppermute | solution.py:584
  320.8 13.9 %collective-permute-done.37 = bf16[2,192,384]{2,1,0:T(8,128)(2,1)S(1)} collective-permute-done((bf16[2,192,384]{2,1,0:T(8,128)(2,1)S(1)}, bf16[2,192,384]{2,1,0:T(8,128)(2,1)S(1)}, u32[]{:S(2)}, u32[]{:S(2)}) %collective-permute-start.37) | collective-permute-done | bytes 294944 | tf_op jit(solution)/shard_map/ppermute | solution.py:584
  338.0 3.5 %collective-permute-done.39 = bf16[192,384]{1,0:T(8,128)(2,1)S(1)} collective-permute-done((bf16[192,384]{1,0:T(8,128)(2,1)S(1)}, bf16[192,384]{1,0:T(8,128)(2,1)S(1)}, u32[]{:S(2)}, u32[]{:S(2)}) %collective-permute-start.39) | collective-permute-done | bytes 147488 | tf_op jit(solution)/shard_map/ppermute | solution.py:584
  (235 shorter events, 77.3 us)
Async XLA Ops:
  3.1 22.9 %collective-permute-start.5 = (bf16[2,128,768]{2,1,0:T(8,128)(2,1)S(1)}, bf16[2,128,768]{2,1,0:T(8,128)(2,1)}, u32[]{:S(2)}, u32[]{:S(2)}) collective-permute-start(bf16[2,128,768]{2,1,0:T(8,128)(2,1)S(1)} %get-tuple-element.141), channel_id=1, source_target_pairs={{0,2},{1,3},{2,0},{3,1},{4,6},{5,7},{6,4},{7,5},{8,10},{9,11},{10,... | collective-permute-start | bytes 1179656 | tf_op jit(solution)/shard_map/ppermute | solution.py:584
  6.0 16.8 %collective-permute-start = (bf16[2,128,768]{2,1,0:T(8,128)(2,1)S(1)}, bf16[2,128,768]{2,1,0:T(8,128)(2,1)}, u32[]{:S(2)}, u32[]{:S(2)}) collective-permute-start(bf16[2,128,768]{2,1,0:T(8,128)(2,1)S(1)} %get-tuple-element.143), channel_id=1, source_target_pairs={{0,3},{1,2},{2,1},{3,0},{4,7},{5,6},{6,5},{7,4},{8,11},{9,10},{10,... | collective-permute-start | bytes 1179656 | tf_op jit(solution)/shard_map/ppermute | solution.py:584
  6.0 20.0 %collective-permute-start.4 = (bf16[2,128,768]{2,1,0:T(8,128)(2,1)S(1)}, bf16[2,128,768]{2,1,0:T(8,128)(2,1)}, u32[]{:S(2)}, u32[]{:S(2)}) collective-permute-start(bf16[2,128,768]{2,1,0:T(8,128)(2,1)S(1)} %get-tuple-element.144), channel_id=1, source_target_pairs={{0,1},{1,0},{2,3},{3,2},{4,5},{5,4},{6,7},{7,6},{8,9},{9,8},{10,11... | collective-permute-start | bytes 1179656 | tf_op jit(solution)/shard_map/ppermute | solution.py:584
  23.7 20.1 %collective-permute-start.3 = (bf16[2,128,768]{2,1,0:T(8,128)(2,1)S(1)}, bf16[2,128,768]{2,1,0:T(8,128)(2,1)S(1)}, u32[]{:S(2)}, u32[]{:S(2)}) collective-permute-start(bf16[2,128,768]{2,1,0:T(8,128)(2,1)S(1)} %get-tuple-element.145), channel_id=1, source_target_pairs={{0,3},{1,2},{2,1},{3,0},{4,7},{5,6},{6,5},{7,4},{8,11},{9,10},{10,... | collective-permute-start | bytes 1179656 | tf_op jit(solution)/shard_map/ppermute | solution.py:584
  25.7 18.1 %collective-permute-start.2 = (bf16[2,128,768]{2,1,0:T(8,128)(2,1)S(1)}, bf16[2,128,768]{2,1,0:T(8,128)(2,1)S(1)}, u32[]{:S(2)}, u32[]{:S(2)}) collective-permute-start(bf16[2,128,768]{2,1,0:T(8,128)(2,1)S(1)} %get-tuple-element.146), channel_id=1, source_target_pairs={{0,2},{1,3},{2,0},{3,1},{4,6},{5,7},{6,4},{7,5},{8,10},{9,11},{10,... | collective-permute-start | bytes 1179656 | tf_op jit(solution)/shard_map/ppermute | solution.py:584
  26.0 17.9 %collective-permute-start.1 = (bf16[2,128,768]{2,1,0:T(8,128)(2,1)S(1)}, bf16[2,128,768]{2,1,0:T(8,128)(2,1)S(1)}, u32[]{:S(2)}, u32[]{:S(2)}) collective-permute-start(bf16[2,128,768]{2,1,0:T(8,128)(2,1)S(1)} %get-tuple-element.147), channel_id=1, source_target_pairs={{0,1},{1,0},{2,3},{3,2},{4,5},{5,4},{6,7},{7,6},{8,9},{9,8},{10,11... | collective-permute-start | bytes 1179656 | tf_op jit(solution)/shard_map/ppermute | solution.py:584
  151.5 18.5 %collective-permute-start.26 = (bf16[2,4,2,48,384]{4,3,2,1,0:T(8,128)(2,1)S(1)}, bf16[2,4,2,48,384]{4,3,2,1,0:T(8,128)(2,1)S(1)}, u32[]{:S(2)}, u32[]{:S(2)}) collective-permute-start(bf16[2,4,2,48,384]{4,3,2,1,0:T(8,128)(2,1)S(1)} %copy-done.26), channel_id=1, source_target_pairs={{0,1},{1,0},{2,3},{3,2},{4,5},{5,4},{6,7},{7,6},{8,9},{9,8},{10,11... | collective-permute-start | bytes 1769480 | tf_op jit(solution)/shard_map/ppermute | solution.py:584
  164.0 43.0 %collective-permute-start.12 = (bf16[3,2,4,2,48,384]{5,4,3,2,1,0:T(8,128)(2,1)}, bf16[3,2,4,2,48,384]{5,4,3,2,1,0:T(8,128)(2,1)S(1)}, u32[]{:S(2)}, u32[]{:S(2)}) collective-permute-start(bf16[3,2,4,2,48,384]{5,4,3,2,1,0:T(8,128)(2,1)} %get-tuple-element.78), channel_id=1, source_target_pairs={{0,1},{1,0},{2,3},{3,2},{4,5},{5,4},{6,7},{7,6},{8,9},{9,8},{10,11... | collective-permute-start | bytes 5308424 | tf_op jit(solution)/shard_map/ppermute | solution.py:584
  171.7 62.1 %collective-permute-start.40 = (bf16[2,4,2,96,768]{4,3,2,1,0:T(8,128)(2,1)}, bf16[2,4,2,96,768]{4,3,2,1,0:T(8,128)(2,1)}, u32[]{:S(2)}, u32[]{:S(2)}) collective-permute-start(bf16[2,4,2,96,768]{4,3,2,1,0:T(8,128)(2,1)} %get-tuple-element.92), channel_id=1, source_target_pairs={{0,1},{1,0},{2,3},{3,2},{4,5},{5,4},{6,7},{7,6},{8,9},{9,8},{10,11... | collective-permute-start | bytes 7077896 | tf_op jit(solution)/shard_map/ppermute | solution.py:584
  175.9 12.1 %collective-permute-start.6 = (bf16[2,128,768]{2,1,0:T(8,128)(2,1)S(1)}, bf16[2,128,768]{2,1,0:T(8,128)(2,1)S(1)}, u32[]{:S(2)}, u32[]{:S(2)}) collective-permute-start(bf16[2,128,768]{2,1,0:T(8,128)(2,1)S(1)} %copy-done.31), channel_id=1, source_target_pairs={{0,1},{1,0},{2,3},{3,2},{4,5},{5,4},{6,7},{7,6},{8,9},{9,8},{10,11... | collective-permute-start | bytes 1179656 | tf_op jit(solution)/shard_map/ppermute | solution.py:584
  176.3 12.3 %collective-permute-start.7 = (bf16[2,128,768]{2,1,0:T(8,128)(2,1)S(1)}, bf16[2,128,768]{2,1,0:T(8,128)(2,1)S(1)}, u32[]{:S(2)}, u32[]{:S(2)}) collective-permute-start(bf16[2,128,768]{2,1,0:T(8,128)(2,1)S(1)} %copy-done.30), channel_id=1, source_target_pairs={{0,2},{1,3},{2,0},{3,1},{4,6},{5,7},{6,4},{7,5},{8,10},{9,11},{10,... | collective-permute-start | bytes 1179656 | tf_op jit(solution)/shard_map/ppermute | solution.py:584
  177.4 9.5 %collective-permute-start.53 = (bf16[32,64]{1,0:T(8,128)(2,1)S(1)}, bf16[32,64]{1,0:T(8,128)(2,1)S(1)}, u32[]{:S(2)}, u32[]{:S(2)}) collective-permute-start(bf16[32,64]{1,0:T(8,128)(2,1)S(1)} %get-tuple-element.189), channel_id=1, source_target_pairs={{0,3},{1,2},{2,1},{3,0},{4,7},{5,6},{6,5},{7,4},{8,11},{9,10},{10,... | collective-permute-start | bytes 12296 | tf_op jit(solution)/shard_map/ppermute | solution.py:584
  188.0 67.8 %collective-permute-start.34 = (bf16[2,4,2,192,384]{4,3,2,1,0:T(8,128)(2,1)}, bf16[2,4,2,192,384]{4,3,2,1,0:T(8,128)(2,1)}, u32[]{:S(2)}, u32[]{:S(2)}) collective-permute-start(bf16[2,4,2,192,384]{4,3,2,1,0:T(8,128)(2,1)} %get-tuple-element.90), channel_id=1, source_target_pairs={{0,1},{1,0},{2,3},{3,2},{4,5},{5,4},{6,7},{7,6},{8,9},{9,8},{10,11... | collective-permute-start | bytes 7077896 | tf_op jit(solution)/shard_map/ppermute | solution.py:584
  194.8 10.7 %collective-permute-start.8 = (bf16[2,128,768]{2,1,0:T(8,128)(2,1)S(1)}, bf16[2,128,768]{2,1,0:T(8,128)(2,1)S(1)}, u32[]{:S(2)}, u32[]{:S(2)}) collective-permute-start(bf16[2,128,768]{2,1,0:T(8,128)(2,1)S(1)} %copy-done.27), channel_id=1, source_target_pairs={{0,3},{1,2},{2,1},{3,0},{4,7},{5,6},{6,5},{7,4},{8,11},{9,10},{10,... | collective-permute-start | bytes 1179656 | tf_op jit(solution)/shard_map/ppermute | solution.py:584
  205.5 12.3 %collective-permute-start.10 = (bf16[2,128,768]{2,1,0:T(8,128)(2,1)}, bf16[2,128,768]{2,1,0:T(8,128)(2,1)S(1)}, u32[]{:S(2)}, u32[]{:S(2)}) collective-permute-start(bf16[2,128,768]{2,1,0:T(8,128)(2,1)} %get-tuple-element.75), channel_id=1, source_target_pairs={{0,2},{1,3},{2,0},{3,1},{4,6},{5,7},{6,4},{7,5},{8,10},{9,11},{10,... | collective-permute-start | bytes 1179656 | tf_op jit(solution)/shard_map/ppermute | solution.py:584
  206.8 17.4 %collective-permute-start.11 = (bf16[2,128,768]{2,1,0:T(8,128)(2,1)S(1)}, bf16[2,128,768]{2,1,0:T(8,128)(2,1)S(1)}, u32[]{:S(2)}, u32[]{:S(2)}) collective-permute-start(bf16[2,128,768]{2,1,0:T(8,128)(2,1)S(1)} %copy-done.28), channel_id=1, source_target_pairs={{0,3},{1,2},{2,1},{3,0},{4,7},{5,6},{6,5},{7,4},{8,11},{9,10},{10,... | collective-permute-start | bytes 1179656 | tf_op jit(solution)/shard_map/ppermute | solution.py:584
  207.0 19.2 %collective-permute-start.31 = (bf16[48,192]{1,0:T(8,128)(2,1)S(1)}, bf16[48,192]{1,0:T(8,128)(2,1)S(1)}, u32[]{:S(2)}, u32[]{:S(2)}) collective-permute-start(bf16[48,192]{1,0:T(8,128)(2,1)S(1)} %get-tuple-element.175), channel_id=1, source_target_pairs={{0,2},{1,3},{2,0},{3,1},{4,6},{5,7},{6,4},{7,5},{8,10},{9,11},{10,... | collective-permute-start | bytes 55304 | tf_op jit(solution)/shard_map/ppermute | solution.py:584
  217.8 15.6 %collective-permute-start.32 = (bf16[48,192]{1,0:T(8,128)(2,1)S(1)}, bf16[48,192]{1,0:T(8,128)(2,1)S(1)}, u32[]{:S(2)}, u32[]{:S(2)}) collective-permute-start(bf16[48,192]{1,0:T(8,128)(2,1)S(1)} %get-tuple-element.176), channel_id=1, source_target_pairs={{0,1},{1,0},{2,3},{3,2},{4,5},{5,4},{6,7},{7,6},{8,9},{9,8},{10,11... | collective-permute-start | bytes 55304 | tf_op jit(solution)/shard_map/ppermute | solution.py:584
  224.2 9.1 %collective-permute-start.33 = (bf16[48,192]{1,0:T(8,128)(2,1)S(1)}, bf16[48,192]{1,0:T(8,128)(2,1)S(1)}, u32[]{:S(2)}, u32[]{:S(2)}) collective-permute-start(bf16[48,192]{1,0:T(8,128)(2,1)S(1)} %get-tuple-element.177), channel_id=1, source_target_pairs={{0,3},{1,2},{2,1},{3,0},{4,7},{5,6},{6,5},{7,4},{8,11},{9,10},{10,... | collective-permute-start | bytes 55304 | tf_op jit(solution)/shard_map/ppermute | solution.py:584
  226.1 22.9 %collective-permute-start.13 = (bf16[3,4,2,48,384]{4,3,2,1,0:T(8,128)(2,1)}, bf16[3,4,2,48,384]{4,3,2,1,0:T(8,128)(2,1)}, u32[]{:S(2)}, u32[]{:S(2)}) collective-permute-start(bf16[3,4,2,48,384]{4,3,2,1,0:T(8,128)(2,1)} %fusion.3), channel_id=1, source_target_pairs={{0,4},{4,0},{8,12},{12,8},{16,20},{20,16},{24,28},{28,24},{1,5},{5... | collective-permute-start | bytes 2654216 | tf_op jit(solution)/shard_map/ppermute | solution.py:584
  238.6 38.5 %collective-permute-start.41 = (bf16[4,2,96,768]{3,2,1,0:T(8,128)(2,1)}, bf16[4,2,96,768]{3,2,1,0:T(8,128)(2,1)}, u32[]{:S(2)}, u32[]{:S(2)}) collective-permute-start(bf16[4,2,96,768]{3,2,1,0:T(8,128)(2,1)} %get-tuple-element.130), channel_id=1, source_target_pairs={{0,4},{4,0},{8,12},{12,8},{16,20},{20,16},{24,28},{28,24},{1,5},{5... | collective-permute-start | bytes 3538952 | tf_op jit(solution)/shard_map/ppermute | solution.py:584
  250.0 10.8 %collective-permute-start.16 = (bf16[3,2,48,384]{3,2,1,0:T(8,128)(2,1)S(1)}, bf16[3,2,48,384]{3,2,1,0:T(8,128)(2,1)S(1)}, u32[]{:S(2)}, u32[]{:S(2)}) collective-permute-start(bf16[3,2,48,384]{3,2,1,0:T(8,128)(2,1)S(1)} %fusion.35), channel_id=1, source_target_pairs={{0,24},{4,28},{8,16},{12,20},{16,8},{20,12},{24,0},{28,4},{1,25},{... | collective-permute-start | bytes 663560 | tf_op jit(solution)/shard_map/ppermute | solution.py:584
  253.1 9.2 %collective-permute-start.14 = (bf16[3,2,48,384]{3,2,1,0:T(8,128)(2,1)S(1)}, bf16[3,2,48,384]{3,2,1,0:T(8,128)(2,1)S(1)}, u32[]{:S(2)}, u32[]{:S(2)}) collective-permute-start(bf16[3,2,48,384]{3,2,1,0:T(8,128)(2,1)S(1)} %get-tuple-element.139), channel_id=1, source_target_pairs={{0,8},{4,12},{8,0},{12,4},{16,24},{20,28},{24,16},{28,20},{1,9},{5... | collective-permute-start | bytes 663560 | tf_op jit(solution)/shard_map/ppermute | solution.py:584
  255.3 15.0 %collective-permute-start.15 = (bf16[3,2,48,384]{3,2,1,0:T(8,128)(2,1)S(1)}, bf16[3,2,48,384]{3,2,1,0:T(8,128)(2,1)S(1)}, u32[]{:S(2)}, u32[]{:S(2)}) collective-permute-start(bf16[3,2,48,384]{3,2,1,0:T(8,128)(2,1)S(1)} %get-tuple-element.140), channel_id=1, source_target_pairs={{0,16},{4,20},{8,24},{12,28},{16,0},{20,4},{24,8},{28,12},{1,17},{... | collective-permute-start | bytes 663560 | tf_op jit(solution)/shard_map/ppermute | solution.py:584
  259.2 38.8 %collective-permute-start.35 = (bf16[4,2,192,384]{3,2,1,0:T(8,128)(2,1)}, bf16[4,2,192,384]{3,2,1,0:T(8,128)(2,1)}, u32[]{:S(2)}, u32[]{:S(2)}) collective-permute-start(bf16[4,2,192,384]{3,2,1,0:T(8,128)(2,1)} %get-tuple-element.132), channel_id=1, source_target_pairs={{0,4},{4,0},{8,12},{12,8},{16,20},{20,16},{24,28},{28,24},{1,5},{5... | collective-permute-start | bytes 3538952 | tf_op jit(solution)/shard_map/ppermute | solution.py:584
  279.3 25.4 %collective-permute-start.42 = (bf16[2,96,768]{2,1,0:T(8,128)(2,1)}, bf16[2,96,768]{2,1,0:T(8,128)(2,1)S(1)}, u32[]{:S(2)}, u32[]{:S(2)}) collective-permute-start(bf16[2,96,768]{2,1,0:T(8,128)(2,1)} %get-tuple-element.133), channel_id=1, source_target_pairs={{0,8},{4,12},{8,0},{12,4},{16,24},{20,28},{24,16},{28,20},{1,9},{5... | collective-permute-start | bytes 884744 | tf_op jit(solution)/shard_map/ppermute | solution.py:584
  279.4 25.3 %collective-permute-start.44 = (bf16[2,96,768]{2,1,0:T(8,128)(2,1)}, bf16[2,96,768]{2,1,0:T(8,128)(2,1)S(1)}, u32[]{:S(2)}, u32[]{:S(2)}) collective-permute-start(bf16[2,96,768]{2,1,0:T(8,128)(2,1)} %get-tuple-element.134), channel_id=1, source_target_pairs={{0,24},{4,28},{8,16},{12,20},{16,8},{20,12},{24,0},{28,4},{1,25},{... | collective-permute-start | bytes 884744 | tf_op jit(solution)/shard_map/ppermute | solution.py:584
  281.5 29.7 %collective-permute-start.43 = (bf16[2,96,768]{2,1,0:T(8,128)(2,1)}, bf16[2,96,768]{2,1,0:T(8,128)(2,1)S(1)}, u32[]{:S(2)}, u32[]{:S(2)}) collective-permute-start(bf16[2,96,768]{2,1,0:T(8,128)(2,1)} %get-tuple-element.135), channel_id=1, source_target_pairs={{0,16},{4,20},{8,24},{12,28},{16,0},{20,4},{24,8},{28,12},{1,17},{... | collective-permute-start | bytes 884744 | tf_op jit(solution)/shard_map/ppermute | solution.py:584
  299.3 21.5 %collective-permute-start.36 = (bf16[2,192,384]{2,1,0:T(8,128)(2,1)S(1)}, bf16[2,192,384]{2,1,0:T(8,128)(2,1)S(1)}, u32[]{:S(2)}, u32[]{:S(2)}) collective-permute-start(bf16[2,192,384]{2,1,0:T(8,128)(2,1)S(1)} %get-tuple-element.136), channel_id=1, source_target_pairs={{0,8},{4,12},{8,0},{12,4},{16,24},{20,28},{24,16},{28,20},{1,9},{5... | collective-permute-start | bytes 884744 | tf_op jit(solution)/shard_map/ppermute | solution.py:584
  302.4 18.4 %collective-permute-start.38 = (bf16[2,192,384]{2,1,0:T(8,128)(2,1)S(1)}, bf16[2,192,384]{2,1,0:T(8,128)(2,1)S(1)}, u32[]{:S(2)}, u32[]{:S(2)}) collective-permute-start(bf16[2,192,384]{2,1,0:T(8,128)(2,1)S(1)} %get-tuple-element.137), channel_id=1, source_target_pairs={{0,24},{4,28},{8,16},{12,20},{16,8},{20,12},{24,0},{28,4},{1,25},{... | collective-permute-start | bytes 884744 | tf_op jit(solution)/shard_map/ppermute | solution.py:584
  304.7 30.0 %collective-permute-start.37 = (bf16[2,192,384]{2,1,0:T(8,128)(2,1)S(1)}, bf16[2,192,384]{2,1,0:T(8,128)(2,1)S(1)}, u32[]{:S(2)}, u32[]{:S(2)}) collective-permute-start(bf16[2,192,384]{2,1,0:T(8,128)(2,1)S(1)} %get-tuple-element.138), channel_id=1, source_target_pairs={{0,16},{4,20},{8,24},{12,28},{16,0},{20,4},{24,8},{28,12},{1,17},{... | collective-permute-start | bytes 884744 | tf_op jit(solution)/shard_map/ppermute | solution.py:584
  312.4 24.8 %collective-permute-start.45 = (bf16[96,768]{1,0:T(8,128)(2,1)S(1)}, bf16[96,768]{1,0:T(8,128)(2,1)S(1)}, u32[]{:S(2)}, u32[]{:S(2)}) collective-permute-start(bf16[96,768]{1,0:T(8,128)(2,1)S(1)} %slice_bitcast_fusion.12), channel_id=1, source_target_pairs={{0,2},{1,3},{2,0},{3,1},{4,6},{5,7},{6,4},{7,5},{8,10},{9,11},{10,... | collective-permute-start | bytes 442376 | tf_op jit(solution)/shard_map/ppermute | solution.py:584
  (57 other events, 773.0 us)
